TPU v7x, 256 devices: a whole 4x4x8 slice. The times are simulated.
256 devices in a mesh: gx: 16 (over y_hi, z), gy: 16 (over x, y_lo, core).
Axes of the slice: x: 4, y: 4 (y_hi: 2, y_lo: 2; y = y_hi * 2 + y_lo), z: 8, core: 2. Of those that a mesh axis runs over, the one named last changes fastest.
Arguments:
- velocity: float32 [3, 4, 128, 2048], P(None, None, 'gy', 'gx'), may hold values from -6 to 6
- old_lm: float32 [4, 128, 2048], P(None, 'gy', 'gx'), may hold values from -6 to 6
- old_mm: float32 [4, 128, 2048], P(None, 'gy', 'gx'), may hold values from 0.5 to 4
- offsets: int32 [3, 4, 128, 2048], P(None, None, 'gy', 'gx'), may hold values from -1 to 2, as said below
- fractions: float32 [3, 4, 128, 2048], P(None, None, 'gy', 'gx'), may hold values from 0 to 1
Outputs:
- new_lm: float32 [4, 128, 2048], P(None, 'gy', 'gx')
- new_mm: float32 [4, 128, 2048], P(None, 'gy', 'gx')
- coefficient: float32 [4, 128, 2048], P(None, 'gy', 'gx')
Inputs may be any that keep to these rules, and one draw needn't show every extreme that they name: offsets[0] is the streamwise distance upstream, 0 or 1; offsets[1] is -1 or 0; offsets[2] is the cell's own level or the one below it, kept within 0 to 2.
All inputs are finite; a program needn't handle non-finite values.
Results may differ from a plain program's by a relative error of at most 0.000021.
Values sent between devices are 32-bit elements; how exact they have to be, the bound alone decides.
No kernel may reach another device: no remote copies, remote signals or barrier semaphores. Data moves between devices by JAX's collectives and lax.ppermute only.
A program may use at most 64 MiB of HBM per device.

v0:
```python
import jax
import jax.numpy as jnp
from jax import lax
from jax.sharding import PartitionSpec as P

relax_rate = 0.3
filter_area = 0.63
spacing_z = 0.5
PAIR_FIRST = (0, 1, 2, 0, 0, 1)
PAIR_SECOND = (0, 1, 2, 1, 2, 2)
PAIR_WEIGHT = (1.0, 1.0, 1.0, 2.0, 2.0, 2.0)


def with_halo(cells, sides, width):
    for axis, dim in sides:
        count = lax.axis_size(axis)
        head = lax.slice_in_dim(cells, 0, width, axis=dim)
        tail = lax.slice_in_dim(cells, cells.shape[dim] - width, cells.shape[dim], axis=dim)
        cells = jnp.concatenate(
            [
                lax.ppermute(tail, axis, [(i, (i + 1) % count) for i in range(count)]),
                cells,
                lax.ppermute(head, axis, [((i + 1) % count, i) for i in range(count)]),
            ],
            axis=dim,
        )
    return cells


def vertical_slope(field):
    inner = (field[..., 2:, :, :] - field[..., :-2, :, :]) * (0.5 / spacing_z)
    bottom = (field[..., 1:2, :, :] - field[..., 0:1, :, :]) * (1.0 / spacing_z)
    top = (field[..., -1:, :, :] - field[..., -2:-1, :, :]) * (1.0 / spacing_z)
    return jnp.concatenate([bottom, inner, top], axis=-3)


def smooth(field):
    along = 0.25 * field[..., :-2] + 0.5 * field[..., 1:-1] + 0.25 * field[..., 2:]
    return 0.25 * along[..., :-2, :] + 0.5 * along[..., 1:-1, :] + 0.25 * along[..., 2:, :]


def slopes(field):
    ddx_part = (field[..., 1:-1, 2:] - field[..., 1:-1, :-2]) * 0.5
    ddy_part = (field[..., 2:, 1:-1] - field[..., :-2, 1:-1]) * 0.5
    return (ddx_part, ddy_part, vertical_slope(field[..., 1:-1, 1:-1]))


def strain_parts(gradient):
    parts = jnp.stack(
        [
            0.5 * (gradient[second][first] + gradient[first][second])
            for first, second in zip(PAIR_FIRST, PAIR_SECOND)
        ]
    )
    weights = jnp.array(PAIR_WEIGHT, jnp.float32).reshape(6, 1, 1, 1)
    magnitude = jnp.sqrt(2.0 * jnp.sum(weights * parts * parts, axis=0))
    return (parts, magnitude)


def contract(filtered_products, filtered_vel, filtered_model, strain_f, magnitude_f):
    weights = jnp.array(PAIR_WEIGHT, jnp.float32).reshape(6, 1, 1, 1)
    resolved = filtered_products - jnp.stack(
        [
            filtered_vel[first] * filtered_vel[second]
            for first, second in zip(PAIR_FIRST, PAIR_SECOND)
        ]
    )
    modelled = 2.0 * filter_area * (filtered_model - 4.0 * magnitude_f[None] * strain_f)
    germano_lm = jnp.sum(weights * resolved * modelled, axis=0)
    germano_mm = jnp.sum(weights * modelled * modelled, axis=0)
    return (germano_lm, germano_mm)


def interpolate(extended, offsets, fractions):
    levels = offsets.shape[1]
    span = offsets.shape[2]
    cells = offsets.shape[3]
    width = extended.shape[3]
    stacked = extended.reshape(2, -1)
    col_x = jnp.arange(cells, dtype=jnp.int32)[None, None, :]
    row_y = jnp.arange(span, dtype=jnp.int32)[None, :, None]
    base_x = col_x + 1 - offsets[0]
    base_y = row_y + 1 + offsets[1]
    level = offsets[2]
    total = jnp.zeros((2, levels, span, cells), jnp.float32)
    for step_z in (0, 1):
        for step_y in (0, 1):
            for step_x in (0, 1):
                weight_x = fractions[0] if step_x else 1.0 - fractions[0]
                weight_y = fractions[1] if step_y else 1.0 - fractions[1]
                weight_z = fractions[2] if step_z else 1.0 - fractions[2]
                weight = weight_x * weight_y * weight_z
                flat = ((level + step_z) * (span + 2) + base_y + step_y) * width + base_x + step_x
                picked = jnp.take(stacked, flat.reshape(-1), axis=1).reshape(2, levels, span, cells)
                total = total + weight[None] * picked
    return total


def body(velocity, old_lm, old_mm, offsets, fractions):
    previous = jnp.stack([old_lm, old_mm])
    velocity_pad = with_halo(velocity, (("gx", 3), ("gy", 2)), 2)
    extended = with_halo(previous, (("gx", 3), ("gy", 2)), 1)
    products = jnp.stack(
        [
            velocity_pad[first] * velocity_pad[second]
            for first, second in zip(PAIR_FIRST, PAIR_SECOND)
        ]
    )
    filtered_products = smooth(products[..., 1:-1, 1:-1])
    filtered_cycle = smooth(velocity_pad)
    filtered_vel = filtered_cycle[..., 1:-1, 1:-1]
    strain, magnitude = strain_parts(slopes(velocity_pad))
    filtered_model = smooth(magnitude[None] * strain)
    strain_f, magnitude_f = strain_parts(slopes(filtered_cycle))
    germano_lm, germano_mm = contract(
        filtered_products, filtered_vel, filtered_model, strain_f, magnitude_f
    )
    carried = interpolate(extended, offsets, fractions)
    new_lm = relax_rate * germano_lm + (1.0 - relax_rate) * carried[0]
    new_mm = relax_rate * germano_mm + (1.0 - relax_rate) * carried[1]
    coefficient = jnp.maximum(new_lm, 0.0) / new_mm
    return (new_lm, new_mm, coefficient)


def solution(mesh):
    placed = (
        P(None, None, "gy", "gx"),
        P(None, "gy", "gx"),
        P(None, "gy", "gx"),
        P(None, None, "gy", "gx"),
        P(None, None, "gy", "gx"),
    )
    return jax.shard_map(
        body,
        mesh=mesh,
        in_specs=placed,
        out_specs=(P(None, "gy", "gx"), P(None, "gy", "gx"), P(None, "gy", "gx")),
        check_vma=False,
    )
```

profile of v0, /device:TPU:2, one launch (start us, length us, event | category | flops | bytes accessed | tf_op | source)
XLA Modules:
  0.0 192.5 jit_solution(12142643832080521578)
XLA Ops:
  1.5 8.5 %collective-permute-start.5 = (f32[2,4,8,1]{3,2,1,0:T(8,128)S(1)}, f32[2,4,8,1]{3,2,1,0:T(8,128)S(1)}, u32[]{:S(2)}, u32[]{:S(2)}) collective-permute-start(f32[2,4,8,1]{3,2,1,0:T(8,128)S(1)} %get-tuple-element.44), channel_id=1, source_target_pairs={{16,0},{32,16},{48,32},{64,48},{80,64},{96,80},{112,96},{128,112},... | collective-permute-start | bytes 776 | tf_op jit(solution)/shard_map/ppermute | solution.py:23
  11.0 5.7 %collective-permute-start.1 = (f32[3,4,8,2]{3,2,1,0:T(8,128)S(1)}, f32[3,4,8,2]{3,2,1,0:T(8,128)S(1)}, u32[]{:S(2)}, u32[]{:S(2)}) collective-permute-start(f32[3,4,8,2]{3,2,1,0:T(8,128)S(1)} %get-tuple-element.34), channel_id=1, source_target_pairs={{16,0},{32,16},{48,32},{64,48},{80,64},{96,80},{112,96},{128,112},... | collective-permute-start | bytes 2312 | tf_op jit(solution)/shard_map/ppermute | solution.py:23
  20.7 3.7 %collective-permute-done = f32[3,4,8,2]{3,2,1,0:T(8,128)S(1)} collective-permute-done((f32[3,4,8,2]{3,2,1,0:T(8,128)S(1)}, f32[3,4,8,2]{3,2,1,0:T(8,128)S(1)}, u32[]{:S(2)}, u32[]{:S(2)}) %collective-permute-start) | collective-permute-done | bytes 800 | tf_op jit(solution)/shard_map/ppermute | solution.py:21
  27.8 14.1 %gather_fusion.7 = f32[4096,2]{1,0:T(8,128)} fusion(f32[2,5200]{0,1:T(8,128)S(1)} %copy.20, s32[4096]{0:T(1024)S(1)} %get-tuple-element.52), kind=kCustom, calls=%fused_computation.7.clone | custom fusion | bytes 81920 | tf_op jit(solution)/shard_map/jit(_take)/gather | solution.py:94
  42.0 4.7 %broadcast_select_fusion = f32[4096,2]{1,0:T(8,128)} fusion(f32[4096,2]{1,0:T(8,128)} %gather_fusion.7, pred[4096]{0:T(1024)(128)(4,1)S(1)} %get-tuple-element.57), kind=kLoop, calls=%fused_computation.8 | loop fusion | flops 8192 | bytes 69632 | tf_op jit(solution)/shard_map/jit(_take)/select_n | solution.py:94
  46.7 2.2 %copy.35 = f32[2,4,8,128]{3,2,1,0:T(8,128)S(1)} copy(f32[2,4,8,128]{0,3,2,1:T(8,128)} %bitcast.136) | data formatting | bytes 65536 | tf_op jit(solution)/shard_map/reshape | solution.py:94
  48.9 14.1 %gather_fusion.6 = f32[4096,2]{1,0:T(8,128)} fusion(f32[2,5200]{0,1:T(8,128)S(1)} %copy.20, s32[4096]{0:T(1024)S(1)} %get-tuple-element.51), kind=kCustom, calls=%fused_computation.6.clone | custom fusion | bytes 81920 | tf_op jit(solution)/shard_map/jit(_take)/gather | solution.py:94
  63.0 14.1 %gather_fusion.4 = f32[4096,2]{1,0:T(8,128)} fusion(f32[2,5200]{0,1:T(8,128)S(1)} %copy.20, s32[4096]{0:T(1024)S(1)} %get-tuple-element.49), kind=kCustom, calls=%fused_computation.4.clone | custom fusion | bytes 81920 | tf_op jit(solution)/shard_map/jit(_take)/gather | solution.py:94
  77.1 6.5 %broadcast_select_fusion.1 = (f32[4096,2]{1,0:T(8,128)}, f32[4096,2]{1,0:T(8,128)}) fusion(f32[4096,2]{1,0:T(8,128)} %gather_fusion.6, pred[4096]{0:T(1024)(128)(4,1)S(1)} %get-tuple-element.27, f32[4096,2]{1,0:T(8,128)} %gather_fusion.4, pred[4096]{0:T(1024)(128)(4,1)S(1)} %get-tuple-element.31), kind=kLoop, calls=%fused_computation.9 | loop fusion | flops 16384 | bytes 139264 | tf_op jit(solution)/shard_map/jit(_take)/select_n | solution.py:94
  83.6 2.2 %copy.33 = f32[2,4,8,128]{3,2,1,0:T(8,128)S(1)} copy(f32[2,4,8,128]{0,3,2,1:T(8,128)} %bitcast.134) | data formatting | bytes 65536 | tf_op jit(solution)/shard_map/reshape | solution.py:94
  85.8 14.1 %gather_fusion.5 = f32[4096,2]{1,0:T(8,128)} fusion(f32[2,5200]{0,1:T(8,128)S(1)} %copy.20, s32[4096]{0:T(1024)S(1)} %get-tuple-element.50), kind=kCustom, calls=%fused_computation.5.clone | custom fusion | bytes 81920 | tf_op jit(solution)/shard_map/jit(_take)/gather | solution.py:94
  99.9 4.7 %broadcast_select_fusion.2 = f32[4096,2]{1,0:T(8,128)} fusion(f32[4096,2]{1,0:T(8,128)} %gather_fusion.5, pred[4096]{0:T(1024)(128)(4,1)S(1)} %get-tuple-element.58), kind=kLoop, calls=%fused_computation.10 | loop fusion | flops 8192 | bytes 69632 | tf_op jit(solution)/shard_map/jit(_take)/select_n | solution.py:94
  104.6 2.2 %copy.31 = f32[2,4,8,128]{3,2,1,0:T(8,128)S(1)} copy(f32[2,4,8,128]{0,3,2,1:T(8,128)} %bitcast.137) | data formatting | bytes 65536 | tf_op jit(solution)/shard_map/reshape | solution.py:94
  106.8 2.2 %copy.29 = f32[2,4,8,128]{3,2,1,0:T(8,128)S(1)} copy(f32[2,4,8,128]{0,3,2,1:T(8,128)} %bitcast.133) | data formatting | bytes 65536 | tf_op jit(solution)/shard_map/reshape | solution.py:94
  109.0 14.1 %gather_fusion.3 = f32[4096,2]{1,0:T(8,128)} fusion(f32[2,5200]{0,1:T(8,128)S(1)} %copy.20, s32[4096]{0:T(1024)S(1)} %get-tuple-element.48), kind=kCustom, calls=%fused_computation.3.clone | custom fusion | bytes 81920 | tf_op jit(solution)/shard_map/jit(_take)/gather | solution.py:94
  123.2 4.7 %broadcast_select_fusion.4 = f32[4096,2]{1,0:T(8,128)} fusion(f32[4096,2]{1,0:T(8,128)} %gather_fusion.3, pred[4096]{0:T(1024)(128)(4,1)S(1)} %get-tuple-element.59), kind=kLoop, calls=%fused_computation.12 | loop fusion | flops 8192 | bytes 69632 | tf_op jit(solution)/shard_map/jit(_take)/select_n | solution.py:94
  127.9 2.2 %copy.27 = f32[2,4,8,128]{3,2,1,0:T(8,128)S(1)} copy(f32[2,4,8,128]{0,3,2,1:T(8,128)} %bitcast.138) | data formatting | bytes 65536 | tf_op jit(solution)/shard_map/reshape | solution.py:94
  130.1 14.1 %gather_fusion.2 = f32[4096,2]{1,0:T(8,128)} fusion(f32[2,5200]{0,1:T(8,128)S(1)} %copy.20, s32[4096]{0:T(1024)S(1)} %get-tuple-element.47), kind=kCustom, calls=%fused_computation.2.clone | custom fusion | bytes 81920 | tf_op jit(solution)/shard_map/jit(_take)/gather | solution.py:94
  144.2 14.1 %gather_fusion = f32[4096,2]{1,0:T(8,128)} fusion(f32[2,5200]{0,1:T(8,128)S(1)} %copy.20, s32[4096]{0:T(1024)S(1)} %get-tuple-element.45), kind=kCustom, calls=%fused_computation.clone | custom fusion | bytes 81920 | tf_op jit(solution)/shard_map/jit(_take)/gather | solution.py:94
  158.3 6.6 %broadcast_select_fusion.5 = (f32[4096,2]{1,0:T(8,128)}, f32[4096,2]{1,0:T(8,128)}) fusion(f32[4096,2]{1,0:T(8,128)} %gather_fusion.2, pred[4096]{0:T(1024)(128)(4,1)S(1)} %get-tuple-element.29, f32[4096,2]{1,0:T(8,128)} %gather_fusion, pred[4096]{0:T(1024)(128)(4,1)S(1)} %get-tuple-element.9), kind=kLoop, calls=%fused_computation.13 | loop fusion | flops 16384 | bytes 139264 | tf_op jit(solution)/shard_map/jit(_take)/select_n | solution.py:94
  164.9 2.2 %copy.25 = f32[2,4,8,128]{3,2,1,0:T(8,128)S(1)} copy(f32[2,4,8,128]{0,3,2,1:T(8,128)} %bitcast.135) | data formatting | bytes 65536 | tf_op jit(solution)/shard_map/reshape | solution.py:94
  167.1 14.1 %gather_fusion.1 = f32[4096,2]{1,0:T(8,128)} fusion(f32[2,5200]{0,1:T(8,128)S(1)} %copy.20, s32[4096]{0:T(1024)S(1)} %get-tuple-element.46), kind=kCustom, calls=%fused_computation.1.clone | custom fusion | bytes 81920 | tf_op jit(solution)/shard_map/jit(_take)/gather | solution.py:94
  181.2 4.7 %broadcast_select_fusion.6 = f32[4096,2]{1,0:T(8,128)} fusion(f32[4096,2]{1,0:T(8,128)} %gather_fusion.1, pred[4096]{0:T(1024)(128)(4,1)S(1)} %get-tuple-element.60), kind=kLoop, calls=%fused_computation.14 | loop fusion | flops 8192 | bytes 69632 | tf_op jit(solution)/shard_map/jit(_take)/select_n | solution.py:94
  185.9 2.4 %copy.23 = f32[2,4,8,128]{3,2,1,0:T(8,128)S(1)} copy(f32[2,4,8,128]{0,3,2,1:T(8,128)} %bitcast.139) | data formatting | bytes 65536 | tf_op jit(solution)/shard_map/reshape | solution.py:94
  (84 shorter events, 13.2 us)
Async XLA Ops:
  1.5 17.6 %collective-permute-start.5 = (f32[2,4,8,1]{3,2,1,0:T(8,128)S(1)}, f32[2,4,8,1]{3,2,1,0:T(8,128)S(1)}, u32[]{:S(2)}, u32[]{:S(2)}) collective-permute-start(f32[2,4,8,1]{3,2,1,0:T(8,128)S(1)} %get-tuple-element.44), channel_id=1, source_target_pairs={{16,0},{32,16},{48,32},{64,48},{80,64},{96,80},{112,96},{128,112},... | collective-permute-start | bytes 776 | tf_op jit(solution)/shard_map/ppermute | solution.py:23
  10.0 9.1 %collective-permute-start.4 = (f32[2,4,8,1]{3,2,1,0:T(8,128)S(1)}, f32[2,4,8,1]{3,2,1,0:T(8,128)S(1)}, u32[]{:S(2)}, u32[]{:S(2)}) collective-permute-start(f32[2,4,8,1]{3,2,1,0:T(8,128)S(1)} %get-tuple-element.43), channel_id=1, source_target_pairs={{0,16},{16,32},{32,48},{48,64},{64,80},{80,96},{96,112},{112,128},... | collective-permute-start | bytes 776 | tf_op jit(solution)/shard_map/ppermute | solution.py:21
  11.0 9.7 %collective-permute-start.1 = (f32[3,4,8,2]{3,2,1,0:T(8,128)S(1)}, f32[3,4,8,2]{3,2,1,0:T(8,128)S(1)}, u32[]{:S(2)}, u32[]{:S(2)}) collective-permute-start(f32[3,4,8,2]{3,2,1,0:T(8,128)S(1)} %get-tuple-element.34), channel_id=1, source_target_pairs={{16,0},{32,16},{48,32},{64,48},{80,64},{96,80},{112,96},{128,112},... | collective-permute-start | bytes 2312 | tf_op jit(solution)/shard_map/ppermute | solution.py:23
  16.6 7.8 %collective-permute-start = (f32[3,4,8,2]{3,2,1,0:T(8,128)S(1)}, f32[3,4,8,2]{3,2,1,0:T(8,128)S(1)}, u32[]{:S(2)}, u32[]{:S(2)}) collective-permute-start(f32[3,4,8,2]{3,2,1,0:T(8,128)S(1)} %get-tuple-element.33), channel_id=1, source_target_pairs={{0,16},{16,32},{32,48},{48,64},{64,80},{80,96},{96,112},{112,128},... | collective-permute-start | bytes 2312 | tf_op jit(solution)/shard_map/ppermute | solution.py:21
  20.1 5.9 %collective-permute-start.7 = (f32[2,4,1,130]{3,2,1,0:T(1,128)S(1)}, f32[2,4,1,130]{3,2,1,0:T(1,128)S(1)}, u32[]{:S(2)}, u32[]{:S(2)}) collective-permute-start(f32[2,4,1,130]{3,2,1,0:T(1,128)S(1)} %get-tuple-element.26), channel_id=1, source_target_pairs={{1,0},{2,1},{3,2},{4,3},{5,4},{6,5},{7,6},{8,7},{9,8},{10,9},{11,1... | collective-permute-start | bytes 12488 | tf_op jit(solution)/shard_map/ppermute | solution.py:23
  20.2 5.8 %collective-permute-start.6 = (f32[2,4,1,130]{3,2,1,0:T(1,128)S(1)}, f32[2,4,1,130]{3,2,1,0:T(1,128)S(1)}, u32[]{:S(2)}, u32[]{:S(2)}) collective-permute-start(f32[2,4,1,130]{3,2,1,0:T(1,128)S(1)} %get-tuple-element.25), channel_id=1, source_target_pairs={{0,1},{1,2},{2,3},{3,4},{4,5},{5,6},{6,7},{7,8},{8,9},{9,10},{10,1... | collective-permute-start | bytes 12488 | tf_op jit(solution)/shard_map/ppermute | solution.py:21
  25.4 163.5 %collective-permute-start.3 = (f32[3,4,2,132]{3,2,1,0:T(2,128)S(1)}, f32[3,4,2,132]{3,2,1,0:T(2,128)S(1)}, u32[]{:S(2)}, u32[]{:S(2)}) collective-permute-start(f32[3,4,2,132]{3,2,1,0:T(2,128)S(1)} %get-tuple-element.24), channel_id=1, source_target_pairs={{1,0},{2,1},{3,2},{4,3},{5,4},{6,5},{7,6},{8,7},{9,8},{10,9},{11,1... | collective-permute-start | bytes 38024 | tf_op jit(solution)/shard_map/ppermute | solution.py:23
  25.5 163.4 %collective-permute-start.2 = (f32[3,4,2,132]{3,2,1,0:T(2,128)S(1)}, f32[3,4,2,132]{3,2,1,0:T(2,128)S(1)}, u32[]{:S(2)}, u32[]{:S(2)}) collective-permute-start(f32[3,4,2,132]{3,2,1,0:T(2,128)S(1)} %get-tuple-element.23), channel_id=1, source_target_pairs={{0,1},{1,2},{2,3},{3,4},{4,5},{5,6},{6,7},{7,8},{8,9},{9,10},{10,1... | collective-permute-start | bytes 38024 | tf_op jit(solution)/shard_map/ppermute | solution.py:21
  185.9 2.4 %copy-start = (f32[4096,2]{1,0:T(8,128)S(1)}, f32[4096,2]{1,0:T(8,128)}, u32[]{:S(2)}) copy-start(f32[4096,2]{1,0:T(8,128)} %get-tuple-element.56) | copy-start | bytes 98308
  185.9 3.1 %copy-start.1 = (f32[3,4,8,128]{3,2,1,0:T(8,128)S(1)}, f32[3,4,8,128]{3,2,1,0:T(8,128)}, u32[]{:S(2)}) copy-start(f32[3,4,8,128]{3,2,1,0:T(8,128)} %param.10) | copy-start | bytes 147460
  189.3 1.5 copy-start.2
  190.9 0.9 copy-start.3
where the time goes:
time: 195 us; the launch traced here: 192 us
  local copies, waits for them, and re-layouts  131 us (67%)
  other arithmetic  41.3 us (21%)
  starting transfers between devices  15.3 us (8%)
  waiting for transfers between devices  3.73 us (2%)
    gather x8, local copies, waits for them, and re-layouts, interpolate(): jnp.take(stacked, flat.reshape(-1), axis=1).reshape(2, levels, span, cells)  113 us
    select_n x6, other arithmetic, interpolate(): jnp.take(stacked, flat.reshape(-1), axis=1).reshape(2, levels, span, cells)  31.9 us
    reshape x8, local copies, waits for them, and re-layouts, interpolate(): jnp.take(stacked, flat.reshape(-1), axis=1).reshape(2, levels, span, cells)  16.2 us
    ppermute x4, starting transfers between devices, with_halo(): lax.ppermute(head, axis, [((i + 1) % count, i) for i in range(count)])  14.3 us
  transfers between devices with their start and end apart: 8, of which 1 were waited for; matrix products, arithmetic and copies ran while one was open for 87% of the time, Pallas kernels for 0%

commit v1 on v0

v1 whole, which is shorter than its diff:
```python
import functools

import jax
import jax.numpy as jnp
from jax import lax
from jax.experimental import pallas as pl
from jax.experimental.pallas import tpu as pltpu
from jax.sharding import PartitionSpec as P

relax_rate = 0.3
filter_area = 0.63
spacing_z = 0.5
PAIR_FIRST = (0, 1, 2, 0, 0, 1)
PAIR_SECOND = (0, 1, 2, 1, 2, 2)
LEVELS = 4
ROWS = 8
COLS = 128
PLANES = 3 * LEVELS
OLD = 2 * LEVELS
VMEM = pl.BlockSpec(memory_space=pltpu.VMEM)


def edge_shift(plane):
    return 4 * plane if plane < PLANES else 4 * PLANES + 2 * (plane - PLANES)


def right_mask():
    lane = lax.broadcasted_iota(jnp.int32, (ROWS, COLS), 1)
    step = jnp.where(lane < 4 * PLANES - 2, lane % 4, 2 * (lane % 2))
    return (step < 2) & (lane < 4 * PLANES + 2 * OLD)


def packed_edges(tiles):
    lane = lax.broadcasted_iota(jnp.int32, (ROWS, COLS), 1)
    packed = tiles[0]
    for plane in range(1, PLANES + OLD):
        at = edge_shift(plane)
        first = at - (2 if plane < PLANES else 1)
        packed = jnp.where(lane >= first, pltpu.roll(tiles[plane], at, 1), packed)
    last = edge_shift(0) + COLS - 2
    return jnp.where(lane >= last, tiles[0], packed)


def pack_kernel(vel, old_lm, old_mm, msg_a, msg_b, edges):
    even = 1 - lax.axis_index("gy") % 2
    tiles = []
    for plane in range(PLANES):
        ref = vel.at[plane // LEVELS, plane % LEVELS]
        tiles.append(ref[...])
        msg_a[2 * plane : 2 * plane + 2, :] = ref[pl.ds(6 * even, 2), :]
        msg_b[2 * plane : 2 * plane + 2, :] = ref[pl.ds(6 - 6 * even, 2), :]
    for plane in range(OLD):
        ref = (old_lm, old_mm)[plane // LEVELS].at[plane % LEVELS]
        tiles.append(ref[...])
        msg_a[2 * PLANES + plane : 2 * PLANES + plane + 1, :] = ref[pl.ds(7 * even, 1), :]
        msg_b[2 * PLANES + plane : 2 * PLANES + plane + 1, :] = ref[pl.ds(7 - 7 * even, 1), :]
    edges[...] = packed_edges(tiles)


def rows_kernel(got_a, got_b, own_edges, outer, edges):
    even = lax.axis_index("gy") % 2 == 0
    above = jnp.where(even, got_a[...], got_b[...])
    below = jnp.where(even, got_b[...], got_a[...])
    outer[...] = jnp.zeros_like(outer)
    for plane in range(PLANES):
        outer[plane, 0:2, :] = above[2 * plane : 2 * plane + 2]
        outer[plane, 6:8, :] = below[2 * plane : 2 * plane + 2]
    for plane in range(PLANES, PLANES + OLD):
        outer[plane, 0:1, :] = above[PLANES + plane : PLANES + plane + 1]
        outer[plane, 7:8, :] = below[PLANES + plane : PLANES + plane + 1]
    edges[0:ROWS, :] = own_edges[...]
    edges[ROWS:, :] = packed_edges([outer[plane] for plane in range(PLANES + OLD)])


class Shifts:
    def __init__(self):
        shape = (LEVELS, ROWS, COLS)
        lane = lax.broadcasted_iota(jnp.int32, shape, 2)
        row = lax.broadcasted_iota(jnp.int32, shape, 1)
        self.lane_first, self.lane_last = lane == 0, lane == COLS - 1
        self.row_first, self.row_last = row == 0, row == ROWS - 1

    def east(self, here, other):
        return pltpu.roll(jnp.where(self.lane_first, other, here), COLS - 1, 2)

    def west(self, here, other):
        return pltpu.roll(jnp.where(self.lane_last, other, here), 1, 2)

    def north(self, here, other):
        return pltpu.roll(jnp.where(self.row_first, other, here), ROWS - 1, 1)

    def south(self, here, other):
        return pltpu.roll(jnp.where(self.row_last, other, here), 1, 1)


def weighted(low, mid, high):
    return 0.25 * low + 0.5 * mid + 0.25 * high


def vertical_slope(field):
    inner = (field[2:] - field[:-2]) * (0.5 / spacing_z)
    bottom = (field[1:2] - field[0:1]) * (1.0 / spacing_z)
    top = (field[-1:] - field[-2:-1]) * (1.0 / spacing_z)
    return jnp.concatenate([bottom, inner, top], axis=0)


def strain_parts(gradient):
    parts = [
        gradient[a][a] if a == b else 0.5 * (gradient[b][a] + gradient[a][b])
        for a, b in zip(PAIR_FIRST, PAIR_SECOND)
    ]
    total = parts[0] * parts[0] + parts[1] * parts[1] + parts[2] * parts[2]
    cross = parts[3] * parts[3] + parts[4] * parts[4] + parts[5] * parts[5]
    return parts, jnp.sqrt(2.0 * (total + 2.0 * cross))


def main_kernel(
    vel, old_lm, old_mm, offsets, fractions, outer, edges_a, edges_b, new_lm, new_mm, coefficient
):
    sh = Shifts()
    even = lax.axis_index("gx") % 2 == 0
    right = right_mask()
    halves = []
    for half in range(2):
        a = edges_a[half * ROWS : (half + 1) * ROWS, :]
        b = edges_b[half * ROWS : (half + 1) * ROWS, :]
        halves.append(jnp.where(even, jnp.where(right, a, b), jnp.where(right, b, a)))

    def four(first_plane, own):
        side = [
            jnp.stack(
                [
                    pltpu.roll(half, (COLS - edge_shift(first_plane + z)) % COLS, 1)
                    for z in range(LEVELS)
                ]
            )
            for half in halves
        ]
        return own, side[0], outer[first_plane : first_plane + LEVELS], side[1]

    fields = [four(LEVELS * c, vel[c]) for c in range(3)]
    west, east, along = [], [], []
    for tiles in fields:
        own, side, rows, corner = tiles
        west.append([sh.west(own, side), sh.west(side, own), sh.west(rows, corner), sh.west(corner, rows)])
        east.append([sh.east(own, side), sh.east(side, own), sh.east(rows, corner), sh.east(corner, rows)])
        along.append([weighted(west[-1][t], tiles[t], east[-1][t]) for t in range(4)])
    filtered = []
    for c in range(3):
        filtered.append(
            [
                weighted(sh.south(along[c][t], along[c][t ^ 2]), along[c][t], sh.north(along[c][t], along[c][t ^ 2]))
                for t in range(4)
            ]
        )
    modelled = []
    for t in range(4):
        gradient = [
            (
                0.5 * (east[c][t] - west[c][t]),
                0.5 * (sh.north(fields[c][t], fields[c][t ^ 2]) - sh.south(fields[c][t], fields[c][t ^ 2])),
                vertical_slope(fields[c][t]),
            )
            for c in range(3)
        ]
        parts, magnitude = strain_parts(gradient)
        modelled.append([magnitude * part for part in parts])
    own = [filtered[c][0] for c in range(3)]
    gradient = []
    for c in range(3):
        f, side, rows, _ = filtered[c]
        gradient.append(
            (
                0.5 * (sh.east(f, side) - sh.west(f, side)),
                0.5 * (sh.north(f, rows) - sh.south(f, rows)),
                vertical_slope(f),
            )
        )
    parts_f, magnitude_f = strain_parts(gradient)
    lm = mm = 0.0
    for pair, (a, b) in enumerate(zip(PAIR_FIRST, PAIR_SECOND)):
        line, model = [], []
        for t in (0, 2):
            line.append(
                weighted(west[a][t] * west[b][t], fields[a][t] * fields[b][t], east[a][t] * east[b][t])
            )
            here, side = modelled[t][pair], modelled[t + 1][pair]
            model.append(weighted(sh.west(here, side), here, sh.east(here, side)))
        product = weighted(sh.south(*line), line[0], sh.north(*line))
        smooth = weighted(sh.south(*model), model[0], sh.north(*model))
        resolved = product - own[a] * own[b]
        m = 2.0 * filter_area * (smooth - 4.0 * magnitude_f * parts_f[pair])
        weight = 1.0 if a == b else 2.0
        lm = lm + weight * resolved * m
        mm = mm + weight * m * m

    upstream = offsets[0] == 1
    f0, f1, f2 = fractions[0], fractions[1], fractions[2]
    back = offsets[1] == -1
    g0, g1, g2 = 1.0 - f0, 1.0 - f1, 1.0 - f2
    wx = (jnp.where(upstream, g0, 0.0), jnp.where(upstream, f0, g0), jnp.where(upstream, 0.0, f0))
    wy = (jnp.where(back, g1, 0.0), jnp.where(back, f1, g1), jnp.where(back, 0.0, f1))
    level = offsets[2]
    carried = []
    for k, ref in enumerate((old_lm, old_mm)):
        here, side, rows, corner = four(PLANES + LEVELS * k, ref[...])
        columns = [
            (sh.west(here, side), sh.west(rows, corner)),
            (here, rows),
            (sh.east(here, side), sh.east(rows, corner)),
        ]
        nine = [[sh.south(*pair), pair[0], sh.north(*pair)] for pair in columns]
        total = []
        for z in range(LEVELS):
            value = 0.0
            for s in range(max(z - 1, 0), min(z + 2, LEVELS)):
                weight = jnp.where(level[z] == s, g2[z], jnp.where(level[z] == s - 1, f2[z], 0.0))
                plane = 0.0
                for y in range(3):
                    row = wx[0][z] * nine[0][y][s] + wx[1][z] * nine[1][y][s] + wx[2][z] * nine[2][y][s]
                    plane = plane + wy[y][z] * row
                value = value + weight * plane
            total.append(value)
        carried.append(jnp.stack(total))
    lm_out = relax_rate * lm + (1.0 - relax_rate) * carried[0]
    mm_out = relax_rate * mm + (1.0 - relax_rate) * carried[1]
    new_lm[...] = lm_out
    new_mm[...] = mm_out
    coefficient[...] = jnp.maximum(lm_out, 0.0) / mm_out


def f32(*shape):
    return jax.ShapeDtypeStruct(shape, jnp.float32)


def kernel_call(kernel, outs, args):
    return pl.pallas_call(
        kernel,
        out_shape=outs,
        in_specs=[VMEM] * len(args),
        out_specs=[VMEM] * len(outs),
        compiler_params=pltpu.CompilerParams(vmem_limit_bytes=16 * 1024 * 1024),
    )(*args)


def even_pairs(count):
    return [(i, i ^ 1) for i in range(count)]


def odd_pairs(count):
    return [(i, (((i + 1) % count ^ 1) - 1) % count) for i in range(count)]


def body(velocity, old_lm, old_mm, offsets, fractions):
    nx, ny = lax.axis_size("gx"), lax.axis_size("gy")
    rows = 2 * PLANES + OLD
    msg_a, msg_b, own_edges = kernel_call(
        pack_kernel, [f32(rows, COLS), f32(rows, COLS), f32(ROWS, COLS)], (velocity, old_lm, old_mm)
    )
    got_a = lax.ppermute(msg_a, "gy", even_pairs(ny))
    got_b = lax.ppermute(msg_b, "gy", odd_pairs(ny))
    outer, edges = kernel_call(
        rows_kernel, [f32(PLANES + OLD, ROWS, COLS), f32(2 * ROWS, COLS)], (got_a, got_b, own_edges)
    )
    edges_a = lax.ppermute(edges, "gx", even_pairs(nx))
    edges_b = lax.ppermute(edges, "gx", odd_pairs(nx))
    out = f32(LEVELS, ROWS, COLS)
    return tuple(
        kernel_call(
            main_kernel,
            [out, out, out],
            (velocity, old_lm, old_mm, offsets, fractions, outer, edges_a, edges_b),
        )
    )


def solution(mesh):
    placed = (
        P(None, None, "gy", "gx"),
        P(None, "gy", "gx"),
        P(None, "gy", "gx"),
        P(None, None, "gy", "gx"),
        P(None, None, "gy", "gx"),
    )
    return jax.shard_map(
        body,
        mesh=mesh,
        in_specs=placed,
        out_specs=(P(None, "gy", "gx"), P(None, "gy", "gx"), P(None, "gy", "gx")),
        check_vma=False,
    )
```

time: 195 us -> 21.9 us (0.11); the launches traced: 192 us -> 21.6 us
  local copies, waits for them, and re-layouts: 131 us -> 3.03 us
  other arithmetic: 41.3 us -> 0 us
  starting transfers between devices: 15.3 us -> 10.3 us
  waiting for transfers between devices: 3.73 us -> 6.15 us
    gather x8 -> x0, local copies, waits for them, and re-layouts: 113 us -> none  [interpolate(): jnp.take(stacked, flat.reshape(-1), axis=1).reshape(2, levels, span, cells)]
    select_n x6 -> x0, other arithmetic: 31.9 us -> none  [interpolate(): jnp.take(stacked, flat.reshape(-1), axis=1).reshape(2, levels, span, cells)]
    reshape x10 -> x0, local copies, waits for them, and re-layouts: 17.2 us -> none  [the longest x8 16.2 us: interpolate(): jnp.take(stacked, flat.reshape(-1), axis=1).reshape(2, levels, span, cells)]
    ppermute x8 -> x4, starting transfers between devices: 15.3 us -> 10.3 us  [the longest x1 8.57 us: body(): edges_b = lax.ppermute(edges, 'gx', odd_pairs(nx))]
    unnamed x8 -> x12, local copies, waits for them, and re-layouts: 0.02 us -> 3.03 us
    ppermute x8 -> x4, waiting for transfers between devices: 3.73 us -> 6.15 us  [the longest x1 2.5 us: body(): got_b = lax.ppermute(msg_b, 'gy', odd_pairs(ny))]
    mul x8 -> x0, other arithmetic: 2.21 us -> none  [the longest x2 1.53 us: interpolate(): total = total + weight[None] * picked]
  transfers between devices with their start and end apart: 8 -> 4, of which waited for: 1 -> 3; matrix products, arithmetic and copies ran while one was open for 87% -> 0% of each run, Pallas kernels for 0% -> 0%
where the time goes in v1:
time: 21.9 us; the launch traced here: 21.6 us
  starting transfers between devices  10.3 us (47%)
  waiting for transfers between devices  6.15 us (28%)
  local copies, waits for them, and re-layouts  3.03 us (14%)
  Pallas kernels  1.46 us (7%)
  between operations  0.67 us (3%)
    ppermute x1, starting transfers between devices, body(): edges_b = lax.ppermute(edges, 'gx', odd_pairs(nx))  8.57 us
    unnamed x12, local copies, waits for them, and re-layouts  3.03 us
    ppermute x1, waiting for transfers between devices, body(): got_b = lax.ppermute(msg_b, 'gy', odd_pairs(ny))  2.5 us
    ppermute x1, waiting for transfers between devices, body(): edges_a = lax.ppermute(edges, 'gx', even_pairs(nx))  2.02 us
    ppermute x1, starting transfers between devices, body(): got_b = lax.ppermute(msg_b, 'gy', odd_pairs(ny))  1.65 us
    ppermute x1, waiting for transfers between devices, body(): edges_b = lax.ppermute(edges, 'gx', odd_pairs(nx))  1.63 us
    pallas_call x3, Pallas kernels, kernel_call(): pl.pallas_call(kernel, out_shape=outs, in_specs=[VMEM] * len(args), out_s...  1.46 us
  transfers between devices with their start and end apart: 4, of which 3 were waited for; matrix products, arithmetic and copies ran while one was open for 0% of the time, Pallas kernels for 0%

profile of v1, /device:TPU:2, one launch (start us, length us, event | category | flops | bytes accessed | tf_op | source)
XLA Modules:
  0.0 21.6 jit_solution(12797329601563143901)
XLA Ops:
  0.6 0.0 copy-start
  0.6 0.8 %copy-done = f32[3,4,8,128]{3,2,1,0:T(8,128)S(1)} copy-done((f32[3,4,8,128]{3,2,1,0:T(8,128)S(1)}, f32[3,4,8,128]{3,2,1,0:T(8,128)}, u32[]{:S(2)}) %copy-start) | copy-done | bytes 49176
  1.4 0.0 copy-start.2
  1.4 0.7 %copy-done.2 = f32[4,8,128]{2,1,0:T(8,128)S(1)} copy-done((f32[4,8,128]{2,1,0:T(8,128)S(1)}, f32[4,8,128]{2,1,0:T(8,128)}, u32[]{:S(2)}) %copy-start.2) | copy-done | bytes 16408
  2.1 0.0 copy-start.3
  2.2 0.7 %copy-done.3 = f32[4,8,128]{2,1,0:T(8,128)S(1)} copy-done((f32[4,8,128]{2,1,0:T(8,128)S(1)}, f32[4,8,128]{2,1,0:T(8,128)}, u32[]{:S(2)}) %copy-start.3) | copy-done | bytes 16408
  2.9 0.0 copy-start.1
  2.9 0.0 copy-start.4
  2.9 0.1 shard_map.76
  3.0 0.1 collective-permute-start
  3.1 1.6 %collective-permute-start.1 = (f32[32,128]{1,0:T(8,128)S(1)}, f32[32,128]{1,0:T(8,128)S(1)}, u32[]{:S(2)}, u32[]{:S(2)}) collective-permute-start(f32[32,128]{1,0:T(8,128)S(1)} %get-tuple-element.9), channel_id=1, source_target_pairs={{0,15},{1,2},{2,1},{3,4},{4,3},{5,6},{6,5},{7,8},{8,7},{9,10},{10,... | collective-permute-start | bytes 49160 | tf_op jit(solution)/shard_map/ppermute | solution.py:261
  4.7 0.0 collective-permute-done.got_a
  4.7 2.5 %collective-permute-done.1.got_b = f32[32,128]{1,0:T(8,128)S(1)} collective-permute-done((f32[32,128]{1,0:T(8,128)S(1)}, f32[32,128]{1,0:T(8,128)S(1)}, u32[]{:S(2)}, u32[]{:S(2)}) %collective-permute-start.1) | collective-permute-done | bytes 16416 | tf_op jit(solution)/shard_map/ppermute | solution.py:261
  7.2 0.1 shard_map.77
  7.3 8.6 %collective-permute-start.3 = (f32[16,128]{1,0:T(8,128)S(1)}, f32[16,128]{1,0:T(8,128)S(1)}, u32[]{:S(2)}, u32[]{:S(2)}) collective-permute-start(f32[16,128]{1,0:T(8,128)S(1)} %get-tuple-element.12), channel_id=1, source_target_pairs={{0,240},{16,32},{32,16},{48,64},{64,48},{80,96},{96,80},{112,128},... | collective-permute-start | bytes 24584 | tf_op jit(solution)/shard_map/ppermute | solution.py:266
  15.9 0.0 collective-permute-start.2
  15.9 1.6 %collective-permute-done.3.edges_b = f32[16,128]{1,0:T(8,128)S(1)} collective-permute-done((f32[16,128]{1,0:T(8,128)S(1)}, f32[16,128]{1,0:T(8,128)S(1)}, u32[]{:S(2)}, u32[]{:S(2)}) %collective-permute-start.3) | collective-permute-done | bytes 8224 | tf_op jit(solution)/shard_map/ppermute | solution.py:266
  17.5 2.0 %collective-permute-done.2.edges_a = f32[16,128]{1,0:T(8,128)S(1)} collective-permute-done((f32[16,128]{1,0:T(8,128)S(1)}, f32[16,128]{1,0:T(8,128)S(1)}, u32[]{:S(2)}, u32[]{:S(2)}) %collective-permute-start.2) | collective-permute-done | bytes 8224 | tf_op jit(solution)/shard_map/ppermute | solution.py:265
  19.5 0.0 copy-done.1
  19.5 0.0 copy-done.4
  19.5 0.0 copy-start.5
  19.5 0.8 %copy-done.5 = f32[3,4,8,128]{3,2,1,0:T(8,128)S(1)} copy-done((f32[3,4,8,128]{3,2,1,0:T(8,128)S(1)}, f32[3,4,8,128]{3,2,1,0:T(8,128)}, u32[]{:S(2)}) %copy-start.5) | copy-done | bytes 49176
  20.3 1.3 %shard_map.78 = (f32[4,8,128]{2,1,0:T(8,128)}, f32[4,8,128]{2,1,0:T(8,128)}, f32[4,8,128]{2,1,0:T(8,128)}) custom-call(f32[3,4,8,128]{3,2,1,0:T(8,128)S(1)} %copy-done.1, f32[4,8,128]{2,1,0:T(8,128)S(1)} %copy-done.2, f32[4,8,128]{2,1,0:T(8,128)S(1)} %copy-done.3, s32[3,4,8,128]{3,2,1,0:T(8,128)S(1)} %copy-done.4, f32[3,4,8,128]{3,2,1,0:T(8,128)S(1)} %copy-done.5, ...), custom_call_target="tpu_custom_call" | custom-call | tf_op jit(solution)/shard_map/pallas_call | solution.py:237
Async XLA Ops:
  0.6 0.8 %copy-start = (f32[3,4,8,128]{3,2,1,0:T(8,128)S(1)}, f32[3,4,8,128]{3,2,1,0:T(8,128)}, u32[]{:S(2)}) copy-start(f32[3,4,8,128]{3,2,1,0:T(8,128)} %vel.3) | copy-start | bytes 147460
  1.4 0.7 %copy-start.2 = (f32[4,8,128]{2,1,0:T(8,128)S(1)}, f32[4,8,128]{2,1,0:T(8,128)}, u32[]{:S(2)}) copy-start(f32[4,8,128]{2,1,0:T(8,128)} %old_lm.3) | copy-start | bytes 49156
  2.1 0.7 %copy-start.3 = (f32[4,8,128]{2,1,0:T(8,128)S(1)}, f32[4,8,128]{2,1,0:T(8,128)}, u32[]{:S(2)}) copy-start(f32[4,8,128]{2,1,0:T(8,128)} %old_mm.3) | copy-start | bytes 49156
  2.9 16.7 %copy-start.1 = (f32[3,4,8,128]{3,2,1,0:T(8,128)S(1)}, f32[3,4,8,128]{3,2,1,0:T(8,128)}, u32[]{:S(2)}) copy-start(f32[3,4,8,128]{3,2,1,0:T(8,128)} %vel.3) | copy-start | bytes 147460
  2.9 16.7 %copy-start.4 = (s32[3,4,8,128]{3,2,1,0:T(8,128)S(1)}, s32[3,4,8,128]{3,2,1,0:T(8,128)}, u32[]{:S(2)}) copy-start(s32[3,4,8,128]{3,2,1,0:T(8,128)} %offsets.1) | copy-start | bytes 147460
  3.0 1.8 %collective-permute-start = (f32[32,128]{1,0:T(8,128)S(1)}, f32[32,128]{1,0:T(8,128)S(1)}, u32[]{:S(2)}, u32[]{:S(2)}) collective-permute-start(f32[32,128]{1,0:T(8,128)S(1)} %get-tuple-element.8), channel_id=1, source_target_pairs={{0,1},{1,0},{2,3},{3,2},{4,5},{5,4},{6,7},{7,6},{8,9},{9,8},{10,11... | collective-permute-start | bytes 49160 | tf_op jit(solution)/shard_map/ppermute | solution.py:260
  3.1 4.2 %collective-permute-start.1 = (f32[32,128]{1,0:T(8,128)S(1)}, f32[32,128]{1,0:T(8,128)S(1)}, u32[]{:S(2)}, u32[]{:S(2)}) collective-permute-start(f32[32,128]{1,0:T(8,128)S(1)} %get-tuple-element.9), channel_id=1, source_target_pairs={{0,15},{1,2},{2,1},{3,4},{4,3},{5,6},{6,5},{7,8},{8,7},{9,10},{10,... | collective-permute-start | bytes 49160 | tf_op jit(solution)/shard_map/ppermute | solution.py:261
  7.3 10.2 %collective-permute-start.3 = (f32[16,128]{1,0:T(8,128)S(1)}, f32[16,128]{1,0:T(8,128)S(1)}, u32[]{:S(2)}, u32[]{:S(2)}) collective-permute-start(f32[16,128]{1,0:T(8,128)S(1)} %get-tuple-element.12), channel_id=1, source_target_pairs={{0,240},{16,32},{32,16},{48,64},{64,48},{80,96},{96,80},{112,128},... | collective-permute-start | bytes 24584 | tf_op jit(solution)/shard_map/ppermute | solution.py:266
  15.9 3.7 %collective-permute-start.2 = (f32[16,128]{1,0:T(8,128)S(1)}, f32[16,128]{1,0:T(8,128)S(1)}, u32[]{:S(2)}, u32[]{:S(2)}) collective-permute-start(f32[16,128]{1,0:T(8,128)S(1)} %get-tuple-element.12), channel_id=1, source_target_pairs={{0,16},{16,0},{32,48},{48,32},{64,80},{80,64},{96,112},{112,96},{1... | collective-permute-start | bytes 24584 | tf_op jit(solution)/shard_map/ppermute | solution.py:265
  19.5 0.8 %copy-start.5 = (f32[3,4,8,128]{3,2,1,0:T(8,128)S(1)}, f32[3,4,8,128]{3,2,1,0:T(8,128)}, u32[]{:S(2)}) copy-start(f32[3,4,8,128]{3,2,1,0:T(8,128)} %fractions.1) | copy-start | bytes 147460

commit v2 on v1

--- a/solution.py
+++ b/solution.py
@@ -18,6 +18,7 @@
 PLANES = 3 * LEVELS
 OLD = 2 * LEVELS
 VMEM = pl.BlockSpec(memory_space=pltpu.VMEM)
+HBM = pl.BlockSpec(memory_space=pltpu.HBM)
 
 
 def edge_shift(plane):
@@ -41,8 +42,16 @@
     return jnp.where(lane >= last, tiles[0], packed)
 
 
-def pack_kernel(vel, old_lm, old_mm, msg_a, msg_b, edges):
+def pack_kernel(
+    vel_hbm, lm_hbm, mm_hbm, msg_a, msg_b, edges, vel, old, sems
+):
+    pairs = ((vel_hbm, vel), (lm_hbm, old.at[0]), (mm_hbm, old.at[1]))
+    copies = [pltpu.make_async_copy(*pair, sems.at[k]) for k, pair in enumerate(pairs)]
+    for copy in copies:
+        copy.start()
     even = 1 - lax.axis_index("gy") % 2
+    for copy in copies[:3]:
+        copy.wait()
     tiles = []
     for plane in range(PLANES):
         ref = vel.at[plane // LEVELS, plane % LEVELS]
@@ -50,11 +59,23 @@
         msg_a[2 * plane : 2 * plane + 2, :] = ref[pl.ds(6 * even, 2), :]
         msg_b[2 * plane : 2 * plane + 2, :] = ref[pl.ds(6 - 6 * even, 2), :]
     for plane in range(OLD):
-        ref = (old_lm, old_mm)[plane // LEVELS].at[plane % LEVELS]
+        ref = old.at[plane // LEVELS, plane % LEVELS]
         tiles.append(ref[...])
-        msg_a[2 * PLANES + plane : 2 * PLANES + plane + 1, :] = ref[pl.ds(7 * even, 1), :]
-        msg_b[2 * PLANES + plane : 2 * PLANES + plane + 1, :] = ref[pl.ds(7 - 7 * even, 1), :]
+        at = 2 * PLANES + plane
+        msg_a[at : at + 1, :] = ref[pl.ds(7 * even, 1), :]
+        msg_b[at : at + 1, :] = ref[pl.ds(7 - 7 * even, 1), :]
     edges[...] = packed_edges(tiles)
+
+
+def hold_kernel(off_hbm, frac_hbm, _, off, frac, sems):
+    copies = [
+        pltpu.make_async_copy(off_hbm, off, sems.at[0]),
+        pltpu.make_async_copy(frac_hbm, frac, sems.at[1]),
+    ]
+    for copy in copies:
+        copy.start()
+    for copy in copies:
+        copy.wait()
 
 
 def rows_kernel(got_a, got_b, own_edges, outer, edges):
@@ -233,13 +254,14 @@
     return jax.ShapeDtypeStruct(shape, jnp.float32)
 
 
-def kernel_call(kernel, outs, args):
+def kernel_call(kernel, outs, args, space=VMEM, scratch=(), limit=16 * 1024):
     return pl.pallas_call(
         kernel,
         out_shape=outs,
-        in_specs=[VMEM] * len(args),
+        in_specs=[space] * len(args) if isinstance(space, pl.BlockSpec) else space,
         out_specs=[VMEM] * len(outs),
-        compiler_params=pltpu.CompilerParams(vmem_limit_bytes=16 * 1024 * 1024),
+        scratch_shapes=scratch,
+        compiler_params=pltpu.CompilerParams(vmem_limit_bytes=limit * 1024),
     )(*args)
 
 
@@ -255,10 +277,27 @@
     nx, ny = lax.axis_size("gx"), lax.axis_size("gy")
     rows = 2 * PLANES + OLD
     msg_a, msg_b, own_edges = kernel_call(
-        pack_kernel, [f32(rows, COLS), f32(rows, COLS), f32(ROWS, COLS)], (velocity, old_lm, old_mm)
+        pack_kernel,
+        [f32(rows, COLS), f32(rows, COLS), f32(ROWS, COLS)],
+        (velocity, old_lm, old_mm),
+        space=HBM,
+        scratch=[
+            pltpu.VMEM((3, LEVELS, ROWS, COLS), jnp.float32),
+            pltpu.VMEM((2, LEVELS, ROWS, COLS), jnp.float32),
+            pltpu.SemaphoreType.DMA((3,)),
+        ],
+        limit=55190,
     )
     got_a = lax.ppermute(msg_a, "gy", even_pairs(ny))
     got_b = lax.ppermute(msg_b, "gy", odd_pairs(ny))
+    offsets, fractions = kernel_call(
+        hold_kernel,
+        [jax.ShapeDtypeStruct(offsets.shape, offsets.dtype), f32(3, LEVELS, ROWS, COLS)],
+        (offsets, fractions, own_edges),
+        space=[HBM, HBM, VMEM],
+        scratch=[pltpu.SemaphoreType.DMA((2,))],
+        limit=55116,
+    )
     outer, edges = kernel_call(
         rows_kernel, [f32(PLANES + OLD, ROWS, COLS), f32(2 * ROWS, COLS)], (got_a, got_b, own_edges)
     )

time: 21.9 us -> 19.7 us (0.90)
  local copies, waits for them, and re-layouts: 3.03 us -> 0.01 us
  Pallas kernels: 1.46 us -> 3.18 us
  waiting for transfers between devices: 6.15 us -> 5.28 us
    unnamed x12 -> x6, local copies, waits for them, and re-layouts: 3.03 us -> 0.01 us
    pallas_call x3 -> x4, Pallas kernels: 1.46 us -> 3.18 us  [kernel_call(): pl.pallas_call(kernel, out_shape=outs, in_specs=[space] * len(args) if is...]
    ppermute x1, waiting for transfers between devices: 1.63 us -> 0.76 us  [body(): edges_b = lax.ppermute(edges, 'gx', odd_pairs(nx))]
  transfers between devices with their start and end apart: 4 -> 4, of which waited for: 3 -> 3; matrix products, arithmetic and copies ran while one was open for 0% -> 0% of each run, Pallas kernels for 0% -> 4%
where the time goes in v2:
time: 19.7 us; the launch traced here: 19.5 us
  starting transfers between devices  10.3 us (52%)
  waiting for transfers between devices  5.28 us (27%)
  Pallas kernels  3.18 us (16%)
  between operations  0.68 us (3%)
    ppermute x1, starting transfers between devices, body(): edges_b = lax.ppermute(edges, 'gx', odd_pairs(nx))  8.57 us
    pallas_call x4, Pallas kernels, kernel_call(): pl.pallas_call(kernel, out_shape=outs, in_specs=[space] * len(args) if is...  3.18 us
    ppermute x1, waiting for transfers between devices, body(): got_b = lax.ppermute(msg_b, 'gy', odd_pairs(ny))  2.5 us
    ppermute x1, waiting for transfers between devices, body(): edges_a = lax.ppermute(edges, 'gx', even_pairs(nx))  2.02 us
    ppermute x1, starting transfers between devices, body(): got_b = lax.ppermute(msg_b, 'gy', odd_pairs(ny))  1.65 us
    ppermute x1, waiting for transfers between devices, body(): edges_b = lax.ppermute(edges, 'gx', odd_pairs(nx))  0.76 us
  transfers between devices with their start and end apart: 4, of which 3 were waited for; matrix products, arithmetic and copies ran while one was open for 0% of the time, Pallas kernels for 4%

profile of v2, /device:TPU:2, one launch (start us, length us, event | category | flops | bytes accessed | tf_op | source)
XLA Modules:
  0.0 19.5 jit_solution(10381784233419293260)
XLA Ops:
  0.6 0.9 %shard_map.76 = (f32[32,128]{1,0:T(8,128)S(1)}, f32[32,128]{1,0:T(8,128)S(1)}, f32[8,128]{1,0:T(8,128)S(1)}) custom-call(f32[3,4,8,128]{3,2,1,0:T(8,128)} %vel.1, f32[4,8,128]{2,1,0:T(8,128)} %old_lm.1, f32[4,8,128]{2,1,0:T(8,128)} %old_mm.1), custom_call_target="tpu_custom_call" | custom-call | tf_op jit(solution)/shard_map/pallas_call | solution.py:258
  1.6 0.1 collective-permute-start
  1.7 1.6 %collective-permute-start.1 = (f32[32,128]{1,0:T(8,128)S(1)}, f32[32,128]{1,0:T(8,128)S(1)}, u32[]{:S(2)}, u32[]{:S(2)}) collective-permute-start(f32[32,128]{1,0:T(8,128)S(1)} %get-tuple-element.14), channel_id=1, source_target_pairs={{0,15},{1,2},{2,1},{3,4},{4,3},{5,6},{6,5},{7,8},{8,7},{9,10},{10,... | collective-permute-start | bytes 49160 | tf_op jit(solution)/shard_map/ppermute | solution.py:292
  3.3 0.0 collective-permute-done.got_a
  3.3 2.5 %collective-permute-done.1.got_b = f32[32,128]{1,0:T(8,128)S(1)} collective-permute-done((f32[32,128]{1,0:T(8,128)S(1)}, f32[32,128]{1,0:T(8,128)S(1)}, u32[]{:S(2)}, u32[]{:S(2)}) %collective-permute-start.1) | collective-permute-done | bytes 16416 | tf_op jit(solution)/shard_map/ppermute | solution.py:292
  5.8 0.1 shard_map.78
  5.9 0.0 copy-start
  5.9 8.6 %collective-permute-start.3 = (f32[16,128]{1,0:T(8,128)S(1)}, f32[16,128]{1,0:T(8,128)S(1)}, u32[]{:S(2)}, u32[]{:S(2)}) collective-permute-start(f32[16,128]{1,0:T(8,128)S(1)} %get-tuple-element.16), channel_id=1, source_target_pairs={{0,240},{16,32},{32,16},{48,64},{64,48},{80,96},{96,80},{112,128},... | collective-permute-start | bytes 24584 | tf_op jit(solution)/shard_map/ppermute | solution.py:305
  14.5 0.0 collective-permute-start.2
  14.5 0.0 copy-start.1
  14.5 0.0 copy-start.2
  14.5 0.9 %shard_map.77 = (s32[3,4,8,128]{3,2,1,0:T(8,128)S(1)}, f32[3,4,8,128]{3,2,1,0:T(8,128)S(1)}) custom-call(s32[3,4,8,128]{3,2,1,0:T(8,128)} %off_hbm.1, f32[3,4,8,128]{3,2,1,0:T(8,128)} %frac_hbm.1, f32[8,128]{1,0:T(8,128)S(1)} %get-tuple-element.10._.own_edges), custom_call_target="tpu_custom_call" | custom-call | tf_op jit(solution)/shard_map/pallas_call | solution.py:258
  15.4 0.8 %collective-permute-done.3.edges_b = f32[16,128]{1,0:T(8,128)S(1)} collective-permute-done((f32[16,128]{1,0:T(8,128)S(1)}, f32[16,128]{1,0:T(8,128)S(1)}, u32[]{:S(2)}, u32[]{:S(2)}) %collective-permute-start.3) | collective-permute-done | bytes 8224 | tf_op jit(solution)/shard_map/ppermute | solution.py:305
  16.1 2.0 %collective-permute-done.2.edges_a = f32[16,128]{1,0:T(8,128)S(1)} collective-permute-done((f32[16,128]{1,0:T(8,128)S(1)}, f32[16,128]{1,0:T(8,128)S(1)}, u32[]{:S(2)}, u32[]{:S(2)}) %collective-permute-start.2) | collective-permute-done | bytes 8224 | tf_op jit(solution)/shard_map/ppermute | solution.py:304
  18.2 0.0 copy-done
  18.2 0.0 copy-done.1
  18.2 0.0 copy-done.2
  18.2 1.3 %shard_map.79 = (f32[4,8,128]{2,1,0:T(8,128)}, f32[4,8,128]{2,1,0:T(8,128)}, f32[4,8,128]{2,1,0:T(8,128)}) custom-call(f32[3,4,8,128]{3,2,1,0:T(8,128)S(1)} %copy-done, f32[4,8,128]{2,1,0:T(8,128)S(1)} %copy-done.1, f32[4,8,128]{2,1,0:T(8,128)S(1)} %copy-done.2, s32[3,4,8,128]{3,2,1,0:T(8,128)S(1)} %get-tuple-element.11.offsets, ...), custom_call_target="tpu_custom_call" | custom-call | tf_op jit(solution)/shard_map/pallas_call | solution.py:258
Async XLA Ops:
  1.6 1.8 %collective-permute-start = (f32[32,128]{1,0:T(8,128)S(1)}, f32[32,128]{1,0:T(8,128)S(1)}, u32[]{:S(2)}, u32[]{:S(2)}) collective-permute-start(f32[32,128]{1,0:T(8,128)S(1)} %get-tuple-element.13), channel_id=1, source_target_pairs={{0,1},{1,0},{2,3},{3,2},{4,5},{5,4},{6,7},{7,6},{8,9},{9,8},{10,11... | collective-permute-start | bytes 49160 | tf_op jit(solution)/shard_map/ppermute | solution.py:291
  1.7 4.2 %collective-permute-start.1 = (f32[32,128]{1,0:T(8,128)S(1)}, f32[32,128]{1,0:T(8,128)S(1)}, u32[]{:S(2)}, u32[]{:S(2)}) collective-permute-start(f32[32,128]{1,0:T(8,128)S(1)} %get-tuple-element.14), channel_id=1, source_target_pairs={{0,15},{1,2},{2,1},{3,4},{4,3},{5,6},{6,5},{7,8},{8,7},{9,10},{10,... | collective-permute-start | bytes 49160 | tf_op jit(solution)/shard_map/ppermute | solution.py:292
  5.9 12.2 %copy-start = (f32[3,4,8,128]{3,2,1,0:T(8,128)S(1)}, f32[3,4,8,128]{3,2,1,0:T(8,128)}, u32[]{:S(2)}) copy-start(f32[3,4,8,128]{3,2,1,0:T(8,128)} %vel.1) | copy-start | bytes 147460
  5.9 10.2 %collective-permute-start.3 = (f32[16,128]{1,0:T(8,128)S(1)}, f32[16,128]{1,0:T(8,128)S(1)}, u32[]{:S(2)}, u32[]{:S(2)}) collective-permute-start(f32[16,128]{1,0:T(8,128)S(1)} %get-tuple-element.16), channel_id=1, source_target_pairs={{0,240},{16,32},{32,16},{48,64},{64,48},{80,96},{96,80},{112,128},... | collective-permute-start | bytes 24584 | tf_op jit(solution)/shard_map/ppermute | solution.py:305
  14.5 3.7 %collective-permute-start.2 = (f32[16,128]{1,0:T(8,128)S(1)}, f32[16,128]{1,0:T(8,128)S(1)}, u32[]{:S(2)}, u32[]{:S(2)}) collective-permute-start(f32[16,128]{1,0:T(8,128)S(1)} %get-tuple-element.16), channel_id=1, source_target_pairs={{0,16},{16,0},{32,48},{48,32},{64,80},{80,64},{96,112},{112,96},{1... | collective-permute-start | bytes 24584 | tf_op jit(solution)/shard_map/ppermute | solution.py:304
  14.5 3.7 %copy-start.1 = (f32[4,8,128]{2,1,0:T(8,128)S(1)}, f32[4,8,128]{2,1,0:T(8,128)}, u32[]{:S(2)}) copy-start(f32[4,8,128]{2,1,0:T(8,128)} %old_lm.1) | copy-start | bytes 49156
  14.5 3.7 %copy-start.2 = (f32[4,8,128]{2,1,0:T(8,128)S(1)}, f32[4,8,128]{2,1,0:T(8,128)}, u32[]{:S(2)}) copy-start(f32[4,8,128]{2,1,0:T(8,128)} %old_mm.1) | copy-start | bytes 49156

commit v3 on v2

--- a/solution.py
+++ b/solution.py
@@ -136,16 +136,14 @@
 
 
 def main_kernel(
-    vel, old_lm, old_mm, offsets, fractions, outer, edges_a, edges_b, new_lm, new_mm, coefficient
+    vel, old_lm, old_mm, offsets, fractions, outer, from_right, from_left, new_lm, new_mm, coefficient
 ):
     sh = Shifts()
-    even = lax.axis_index("gx") % 2 == 0
     right = right_mask()
     halves = []
     for half in range(2):
-        a = edges_a[half * ROWS : (half + 1) * ROWS, :]
-        b = edges_b[half * ROWS : (half + 1) * ROWS, :]
-        halves.append(jnp.where(even, jnp.where(right, a, b), jnp.where(right, b, a)))
+        at = slice(half * ROWS, (half + 1) * ROWS)
+        halves.append(jnp.where(right, from_right[at, :], from_left[at, :]))
 
     def four(first_plane, own):
         side = [
@@ -301,14 +299,14 @@
     outer, edges = kernel_call(
         rows_kernel, [f32(PLANES + OLD, ROWS, COLS), f32(2 * ROWS, COLS)], (got_a, got_b, own_edges)
     )
-    edges_a = lax.ppermute(edges, "gx", even_pairs(nx))
-    edges_b = lax.ppermute(edges, "gx", odd_pairs(nx))
+    from_left = lax.ppermute(edges, "gx", [(i, (i + 1) % nx) for i in range(nx)])
+    from_right = lax.ppermute(edges, "gx", [((i + 1) % nx, i) for i in range(nx)])
     out = f32(LEVELS, ROWS, COLS)
     return tuple(
         kernel_call(
             main_kernel,
             [out, out, out],
-            (velocity, old_lm, old_mm, offsets, fractions, outer, edges_a, edges_b),
+            (velocity, old_lm, old_mm, offsets, fractions, outer, from_right, from_left),
         )
     )
 

time: 19.7 us -> 17.6 us (0.89)
  waiting for transfers between devices: 5.28 us -> 3.18 us
    ppermute x2, waiting for transfers between devices: 2.78 us -> 0.68 us  [the longest x1 0.68 us: body(): lax.ppermute(edges, 'gx', [(i, (i + 1) % nx) for i in range(nx)])]
  transfers between devices with their start and end apart: 4 -> 4, of which waited for: 3 -> 2; matrix products, arithmetic and copies ran while one was open for 0% -> 0% of each run, Pallas kernels for 4% -> 5%
where the time goes in v3:
time: 17.6 us; the launch traced here: 17.4 us
  starting transfers between devices  10.4 us (59%)
  waiting for transfers between devices  3.18 us (18%)
  Pallas kernels  3.17 us (18%)
  between operations  0.68 us (4%)
    ppermute x1, starting transfers between devices, body(): lax.ppermute(edges, 'gx', [((i + 1) % nx, i) for i in range(nx)])  6.66 us
    pallas_call x4, Pallas kernels, kernel_call(): pl.pallas_call(kernel, out_shape=outs, in_specs=[space] * len(args) if is...  3.17 us
    ppermute x1, waiting for transfers between devices, body(): got_b = lax.ppermute(msg_b, 'gy', odd_pairs(ny))  2.5 us
    ppermute x1, starting transfers between devices, body(): lax.ppermute(edges, 'gx', [(i, (i + 1) % nx) for i in range(nx)])  1.99 us
    ppermute x1, starting transfers between devices, body(): got_b = lax.ppermute(msg_b, 'gy', odd_pairs(ny))  1.65 us
    ppermute x1, waiting for transfers between devices, body(): lax.ppermute(edges, 'gx', [(i, (i + 1) % nx) for i in range(nx)])  0.68 us
  transfers between devices with their start and end apart: 4, of which 2 were waited for; matrix products, arithmetic and copies ran while one was open for 0% of the time, Pallas kernels for 5%

profile of v3, /device:TPU:2, one launch (start us, length us, event | category | flops | bytes accessed | tf_op | source)
XLA Modules:
  0.0 17.4 jit_solution(12936333576175273794)
XLA Ops:
  0.6 0.9 %shard_map.76 = (f32[32,128]{1,0:T(8,128)S(1)}, f32[32,128]{1,0:T(8,128)S(1)}, f32[8,128]{1,0:T(8,128)S(1)}) custom-call(f32[3,4,8,128]{3,2,1,0:T(8,128)} %vel.1, f32[4,8,128]{2,1,0:T(8,128)} %old_lm.1, f32[4,8,128]{2,1,0:T(8,128)} %old_mm.1), custom_call_target="tpu_custom_call" | custom-call | tf_op jit(solution)/shard_map/pallas_call | solution.py:256
  1.6 0.1 collective-permute-start
  1.7 1.6 %collective-permute-start.1 = (f32[32,128]{1,0:T(8,128)S(1)}, f32[32,128]{1,0:T(8,128)S(1)}, u32[]{:S(2)}, u32[]{:S(2)}) collective-permute-start(f32[32,128]{1,0:T(8,128)S(1)} %get-tuple-element.14), channel_id=1, source_target_pairs={{0,15},{1,2},{2,1},{3,4},{4,3},{5,6},{6,5},{7,8},{8,7},{9,10},{10,... | collective-permute-start | bytes 49160 | tf_op jit(solution)/shard_map/ppermute | solution.py:290
  3.3 0.0 collective-permute-done.got_a
  3.3 2.5 %collective-permute-done.1.got_b = f32[32,128]{1,0:T(8,128)S(1)} collective-permute-done((f32[32,128]{1,0:T(8,128)S(1)}, f32[32,128]{1,0:T(8,128)S(1)}, u32[]{:S(2)}, u32[]{:S(2)}) %collective-permute-start.1) | collective-permute-done | bytes 16416 | tf_op jit(solution)/shard_map/ppermute | solution.py:290
  5.8 0.1 shard_map.78
  5.9 0.0 copy-start
  5.9 2.0 %collective-permute-start.3 = (f32[16,128]{1,0:T(8,128)S(1)}, f32[16,128]{1,0:T(8,128)S(1)}, u32[]{:S(2)}, u32[]{:S(2)}) collective-permute-start(f32[16,128]{1,0:T(8,128)S(1)} %get-tuple-element.16), channel_id=1, source_target_pairs={{0,16},{16,32},{32,48},{48,64},{64,80},{80,96},{96,112},{112,128},... | collective-permute-start | bytes 24584 | tf_op jit(solution)/shard_map/ppermute | solution.py:302
  7.9 6.7 %collective-permute-start.2 = (f32[16,128]{1,0:T(8,128)S(1)}, f32[16,128]{1,0:T(8,128)S(1)}, u32[]{:S(2)}, u32[]{:S(2)}) collective-permute-start(f32[16,128]{1,0:T(8,128)S(1)} %get-tuple-element.16), channel_id=1, source_target_pairs={{16,0},{32,16},{48,32},{64,48},{80,64},{96,80},{112,96},{128,112},... | collective-permute-start | bytes 24584 | tf_op jit(solution)/shard_map/ppermute | solution.py:303
  14.6 0.0 copy-start.1
  14.6 0.0 copy-start.2
  14.6 0.9 %shard_map.77 = (s32[3,4,8,128]{3,2,1,0:T(8,128)S(1)}, f32[3,4,8,128]{3,2,1,0:T(8,128)S(1)}) custom-call(s32[3,4,8,128]{3,2,1,0:T(8,128)} %off_hbm.1, f32[3,4,8,128]{3,2,1,0:T(8,128)} %frac_hbm.1, f32[8,128]{1,0:T(8,128)S(1)} %get-tuple-element.10._.own_edges), custom_call_target="tpu_custom_call" | custom-call | tf_op jit(solution)/shard_map/pallas_call | solution.py:256
  15.5 0.7 %collective-permute-done.3.from_left = f32[16,128]{1,0:T(8,128)S(1)} collective-permute-done((f32[16,128]{1,0:T(8,128)S(1)}, f32[16,128]{1,0:T(8,128)S(1)}, u32[]{:S(2)}, u32[]{:S(2)}) %collective-permute-start.3) | collective-permute-done | bytes 8224 | tf_op jit(solution)/shard_map/ppermute | solution.py:302
  16.1 0.0 collective-permute-done.2.from_right
  16.1 0.0 copy-done
  16.1 0.0 copy-done.1
  16.1 0.0 copy-done.2
  16.2 1.3 %shard_map.79 = (f32[4,8,128]{2,1,0:T(8,128)}, f32[4,8,128]{2,1,0:T(8,128)}, f32[4,8,128]{2,1,0:T(8,128)}) custom-call(f32[3,4,8,128]{3,2,1,0:T(8,128)S(1)} %copy-done, f32[4,8,128]{2,1,0:T(8,128)S(1)} %copy-done.1, f32[4,8,128]{2,1,0:T(8,128)S(1)} %copy-done.2, s32[3,4,8,128]{3,2,1,0:T(8,128)S(1)} %get-tuple-element.11.offsets, ...), custom_call_target="tpu_custom_call" | custom-call | tf_op jit(solution)/shard_map/pallas_call | solution.py:256
Async XLA Ops:
  1.6 1.8 %collective-permute-start = (f32[32,128]{1,0:T(8,128)S(1)}, f32[32,128]{1,0:T(8,128)S(1)}, u32[]{:S(2)}, u32[]{:S(2)}) collective-permute-start(f32[32,128]{1,0:T(8,128)S(1)} %get-tuple-element.13), channel_id=1, source_target_pairs={{0,1},{1,0},{2,3},{3,2},{4,5},{5,4},{6,7},{7,6},{8,9},{9,8},{10,11... | collective-permute-start | bytes 49160 | tf_op jit(solution)/shard_map/ppermute | solution.py:289
  1.7 4.2 %collective-permute-start.1 = (f32[32,128]{1,0:T(8,128)S(1)}, f32[32,128]{1,0:T(8,128)S(1)}, u32[]{:S(2)}, u32[]{:S(2)}) collective-permute-start(f32[32,128]{1,0:T(8,128)S(1)} %get-tuple-element.14), channel_id=1, source_target_pairs={{0,15},{1,2},{2,1},{3,4},{4,3},{5,6},{6,5},{7,8},{8,7},{9,10},{10,... | collective-permute-start | bytes 49160 | tf_op jit(solution)/shard_map/ppermute | solution.py:290
  5.9 10.2 %copy-start = (f32[3,4,8,128]{3,2,1,0:T(8,128)S(1)}, f32[3,4,8,128]{3,2,1,0:T(8,128)}, u32[]{:S(2)}) copy-start(f32[3,4,8,128]{3,2,1,0:T(8,128)} %vel.1) | copy-start | bytes 147460
  5.9 10.2 %collective-permute-start.3 = (f32[16,128]{1,0:T(8,128)S(1)}, f32[16,128]{1,0:T(8,128)S(1)}, u32[]{:S(2)}, u32[]{:S(2)}) collective-permute-start(f32[16,128]{1,0:T(8,128)S(1)} %get-tuple-element.16), channel_id=1, source_target_pairs={{0,16},{16,32},{32,48},{48,64},{64,80},{80,96},{96,112},{112,128},... | collective-permute-start | bytes 24584 | tf_op jit(solution)/shard_map/ppermute | solution.py:302
  7.9 8.2 %collective-permute-start.2 = (f32[16,128]{1,0:T(8,128)S(1)}, f32[16,128]{1,0:T(8,128)S(1)}, u32[]{:S(2)}, u32[]{:S(2)}) collective-permute-start(f32[16,128]{1,0:T(8,128)S(1)} %get-tuple-element.16), channel_id=1, source_target_pairs={{16,0},{32,16},{48,32},{64,48},{80,64},{96,80},{112,96},{128,112},... | collective-permute-start | bytes 24584 | tf_op jit(solution)/shard_map/ppermute | solution.py:303
  14.6 1.5 %copy-start.1 = (f32[4,8,128]{2,1,0:T(8,128)S(1)}, f32[4,8,128]{2,1,0:T(8,128)}, u32[]{:S(2)}) copy-start(f32[4,8,128]{2,1,0:T(8,128)} %old_lm.1) | copy-start | bytes 49156
  14.6 1.6 %copy-start.2 = (f32[4,8,128]{2,1,0:T(8,128)S(1)}, f32[4,8,128]{2,1,0:T(8,128)}, u32[]{:S(2)}) copy-start(f32[4,8,128]{2,1,0:T(8,128)} %old_mm.1) | copy-start | bytes 49156

commit v4 on v3

v4 whole, which is shorter than its diff:
```python
import jax
import jax.numpy as jnp
from jax import lax
from jax.experimental import pallas as pl
from jax.experimental.pallas import tpu as pltpu
from jax.sharding import PartitionSpec as P

relax_rate = 0.3
filter_area = 0.63
spacing_z = 0.5
PAIR_FIRST = (0, 1, 2, 0, 0, 1)
PAIR_SECOND = (0, 1, 2, 1, 2, 2)
LEVELS = 4
ROWS = 8
COLS = 128
FIELDS = 5
PLANES = 3 * LEVELS
OLD = 2 * LEVELS
GROUP = 16
VMEM = pl.BlockSpec(memory_space=pltpu.VMEM)
HBM = pl.BlockSpec(memory_space=pltpu.HBM)


def lanes():
    return lax.broadcasted_iota(jnp.int32, (ROWS, COLS), 1)


def packed_edges(tile):
    lane = lanes()
    packed = None
    for z in range(LEVELS):
        for field in range(FIELDS):
            first = GROUP * z + (4 * field if field < 3 else 12 + 2 * (field - 3))
            moved = pltpu.roll(tile(field, z), first + (2 if field < 3 else 1), 1)
            packed = moved if packed is None else jnp.where(lane >= first, moved, packed)
    return packed


def from_right_mask():
    lane = lanes() % GROUP
    return jnp.where(lane < 12, lane % 4, 2 * (lane % 2)) >= 2


def edge_domain(tile):
    lane = lanes()
    inner = lane % GROUP < 6
    packed = None
    for z in range(LEVELS):
        at = GROUP * z
        plane = tile(z)
        moved = jnp.where(inner, pltpu.roll(plane, at + 4, 1), pltpu.roll(plane, at + 8, 1))
        packed = moved if packed is None else jnp.where(lane >= at, moved, packed)
    return packed


def pack_kernel(vel_hbm, lm_hbm, mm_hbm, msg_a, msg_b, vel, old, sems):
    pairs = ((vel_hbm, vel), (lm_hbm, old.at[0]), (mm_hbm, old.at[1]))
    copies = [pltpu.make_async_copy(*pair, sems.at[k]) for k, pair in enumerate(pairs)]
    for copy in copies:
        copy.start()
    even = 1 - lax.axis_index("gy") % 2
    for copy in copies:
        copy.wait()
    for plane in range(PLANES):
        ref = vel.at[plane // LEVELS, plane % LEVELS]
        msg_a[2 * plane : 2 * plane + 2, :] = ref[pl.ds(6 * even, 2), :]
        msg_b[2 * plane : 2 * plane + 2, :] = ref[pl.ds(6 - 6 * even, 2), :]
    for plane in range(OLD):
        ref = old.at[plane // LEVELS, plane % LEVELS]
        at = 2 * PLANES + plane
        msg_a[at : at + 1, :] = ref[pl.ds(7 * even, 1), :]
        msg_b[at : at + 1, :] = ref[pl.ds(7 - 7 * even, 1), :]


def hold_kernel(
    off_hbm, frac_hbm, vel_hbm, lm_hbm, mm_hbm, _,
    off, frac, edges, near, near_off, near_frac, vel, old, sems,
):
    pairs = (
        (vel_hbm, vel), (lm_hbm, old.at[0]), (mm_hbm, old.at[1]), (off_hbm, off), (frac_hbm, frac)
    )
    copies = [pltpu.make_async_copy(*pair, sems.at[k]) for k, pair in enumerate(pairs)]
    for copy in copies:
        copy.start()
    for copy in copies:
        copy.wait()

    def tile(field, z):
        return vel[field, z] if field < 3 else old[field - 3, z]

    edges[...] = packed_edges(tile)
    for field in range(FIELDS):
        near[field] = edge_domain(lambda z: tile(field, z))
    for k in range(3):
        near_off[k] = edge_domain(lambda z: off[k, z])
        near_frac[k] = edge_domain(lambda z: frac[k, z])


def rows_kernel(got_a, got_b, own_edges, outer, edges):
    even = lax.axis_index("gy") % 2 == 0
    above = jnp.where(even, got_a[...], got_b[...])
    below = jnp.where(even, got_b[...], got_a[...])
    outer[...] = jnp.zeros_like(outer)
    for plane in range(PLANES):
        outer[plane, 0:2, :] = above[2 * plane : 2 * plane + 2]
        outer[plane, 6:8, :] = below[2 * plane : 2 * plane + 2]
    for plane in range(PLANES, PLANES + OLD):
        outer[plane, 0:1, :] = above[PLANES + plane : PLANES + plane + 1]
        outer[plane, 7:8, :] = below[PLANES + plane : PLANES + plane + 1]
    edges[0:ROWS, :] = own_edges[...]
    edges[ROWS:, :] = packed_edges(lambda field, z: outer[LEVELS * field + z])


class Grid:
    def __init__(self, shape=(LEVELS, ROWS, COLS)):
        self.rows = len(shape) - 2
        row = lax.broadcasted_iota(jnp.int32, shape, self.rows)
        self.row_first, self.row_last = row == 0, row == ROWS - 1
        self.level = self.levels(shape)

    def levels(self, shape):
        return lax.broadcasted_iota(jnp.int32, shape, 0)

    def east(self, tile):
        return pltpu.roll(tile, COLS - 1, self.rows + 1)

    def west(self, tile):
        return pltpu.roll(tile, 1, self.rows + 1)

    def north(self, here, other):
        return pltpu.roll(jnp.where(self.row_first, other, here), ROWS - 1, self.rows)

    def south(self, here, other):
        return pltpu.roll(jnp.where(self.row_last, other, here), 1, self.rows)

    def twice_slope(self, field):
        inner = (field[2:] - field[:-2]) * (1.0 / spacing_z)
        bottom = (field[1:2] - field[0:1]) * (2.0 / spacing_z)
        top = (field[-1:] - field[-2:-1]) * (2.0 / spacing_z)
        return jnp.concatenate([bottom, inner, top], axis=0)

    def nine(self, own, rows):
        three = (self.south(own, rows), own, self.north(own, rows))
        return [(self.west(t), t, self.east(t)) for t in three]

    def by_level(self, own, rows):
        here = self.nine(own, rows)
        down = [[jnp.concatenate([t[:1], t[:-1]], axis=0) for t in row] for row in here]
        up = [[jnp.concatenate([t[1:], t[-1:]], axis=0) for t in row] for row in here]
        return down, here, up


class EdgeGrid(Grid):
    def __init__(self):
        super().__init__((ROWS, COLS))

    def levels(self, shape):
        return lanes() // GROUP

    def above(self, tile):
        return pltpu.roll(tile, COLS - GROUP, 1)

    def below(self, tile):
        return pltpu.roll(tile, GROUP, 1)

    def twice_slope(self, field):
        bottom, top = self.level == 0, self.level == LEVELS - 1
        high = jnp.where(top, field, self.above(field))
        low = jnp.where(bottom, field, self.below(field))
        return (high - low) * jnp.where(bottom | top, 2.0 / spacing_z, 1.0 / spacing_z)

    def by_level(self, own, rows):
        return (
            self.nine(self.below(own), self.below(rows)),
            self.nine(own, rows),
            self.nine(self.above(own), self.above(rows)),
        )


def spread(low, mid, high):
    return (low + high) + (mid + mid)


def strains(gradient):
    parts = [
        gradient[a][a] if a == b else gradient[b][a] + gradient[a][b]
        for a, b in zip(PAIR_FIRST, PAIR_SECOND)
    ]
    diagonal = parts[0] * parts[0] + parts[1] * parts[1] + parts[2] * parts[2]
    cross = parts[3] * parts[3] + parts[4] * parts[4] + parts[5] * parts[5]
    return parts, jnp.sqrt((diagonal + diagonal) + cross)


def update(grid, fields, offsets, fractions):
    filtered, gradients = [], []
    for own, rows in fields[:3]:
        tiles = (own, rows)
        west = [grid.west(t) for t in tiles]
        east = [grid.east(t) for t in tiles]
        along = [spread(west[t], tiles[t], east[t]) for t in range(2)]
        filtered.append(
            [
                spread(grid.south(along[t], along[1 - t]), along[t], grid.north(along[t], along[1 - t]))
                for t in range(2)
            ]
        )
        gradients.append(
            [
                (
                    east[t] - west[t],
                    grid.north(tiles[t], tiles[1 - t]) - grid.south(tiles[t], tiles[1 - t]),
                    grid.twice_slope(tiles[t]),
                )
                for t in range(2)
            ]
        )
    modelled = []
    for t in range(2):
        parts, magnitude = strains([gradients[c][t] for c in range(3)])
        modelled.append([magnitude * part for part in parts])
    own_f = [filtered[c][0] for c in range(3)]
    parts_f, magnitude_f = strains(
        [
            (
                grid.east(f) - grid.west(f),
                grid.north(f, rows) - grid.south(f, rows),
                grid.twice_slope(f),
            )
            for f, rows in filtered
        ]
    )

    def both_ways(own, rows):
        t = spread(grid.south(own, rows), own, grid.north(own, rows))
        return spread(grid.west(t), t, grid.east(t))

    product_sum = diagonal = cross = 0.0
    for pair, (a, b) in enumerate(zip(PAIR_FIRST, PAIR_SECOND)):
        product = both_ways(fields[a][0] * fields[b][0], fields[a][1] * fields[b][1])
        resolved = 16.0 * product - own_f[a] * own_f[b]
        smooth = both_ways(modelled[0][pair], modelled[1][pair])
        m = 4.0 * smooth - magnitude_f * parts_f[pair]
        product_sum = product_sum + resolved * m
        if a == b:
            diagonal = diagonal + m * m
        else:
            cross = cross + m * m
    scale = 2.0 * filter_area / 256.0
    lm = product_sum * (scale / 256.0)
    mm = (diagonal + 0.5 * cross) * (scale * scale)

    upstream = offsets[0] == 1
    back = offsets[1] == -1
    at_level, one_below = offsets[2] == grid.level, offsets[2] == grid.level - 1
    f0, f1, f2 = fractions
    g0, g1, g2 = 1.0 - f0, 1.0 - f1, 1.0 - f2
    wx = (jnp.where(upstream, g0, 0.0), jnp.where(upstream, f0, g0), jnp.where(upstream, 0.0, f0))
    wy = (jnp.where(back, g1, 0.0), jnp.where(back, f1, g1), jnp.where(back, 0.0, f1))
    wz = (
        jnp.where(one_below, g2, 0.0),
        jnp.where(at_level, g2, jnp.where(one_below, f2, 0.0)),
        jnp.where(at_level, f2, 0.0),
    )
    results = []
    for germano, (own, rows) in ((lm, fields[3]), (mm, fields[4])):
        carried = 0.0
        for weight, nine in zip(wz, grid.by_level(own, rows)):
            plane = 0.0
            for y in range(3):
                plane = plane + wy[y] * (wx[0] * nine[y][0] + wx[1] * nine[y][1] + wx[2] * nine[y][2])
            carried = carried + weight * plane
        results.append(relax_rate * germano + (1.0 - relax_rate) * carried)
    return results


def inner_kernel(vel, old_lm, old_mm, offsets, fractions, outer, new, near_rows):
    fields = [vel[c] for c in range(3)] + [old_lm[...], old_mm[...]]
    fields = [(own, outer[LEVELS * f : LEVELS * (f + 1)]) for f, own in enumerate(fields)]
    new[0], new[1] = update(Grid(), fields, [offsets[k] for k in range(3)], [fractions[k] for k in range(3)])
    for field in range(FIELDS):
        near_rows[field] = edge_domain(lambda z: outer[LEVELS * field + z])


def edge_kernel(
    inner, near, near_rows, near_off, near_frac, from_right, from_left, new_lm, new_mm, coefficient
):
    right = from_right_mask()
    place = lanes() % GROUP
    is_right, is_left = (place == 4) | (place == 5), (place == 6) | (place == 7)
    pairs = [[], []]
    for half, own in enumerate((near, near_rows)):
        at = slice(half * ROWS, (half + 1) * ROWS)
        halo = jnp.where(right, from_right[at, :], from_left[at, :])
        for field in range(FIELDS):
            first = 4 * field if field < 3 else 12 + 2 * (field - 3)
            to_right = (4 - first - (2 if field < 3 else 1)) % COLS
            to_left = ((6 if field < 3 else 7) - first) % COLS
            tile = jnp.where(is_left, pltpu.roll(halo, to_left, 1), own[field])
            pairs[half].append(jnp.where(is_right, pltpu.roll(halo, to_right, 1), tile))
    fields = list(zip(*pairs))
    edge = update(EdgeGrid(), fields, [near_off[k] for k in range(3)], [near_frac[k] for k in range(3)])
    lane = lanes()
    for z in range(LEVELS):
        out = []
        for k in range(2):
            low = pltpu.roll(edge[k], (COLS - GROUP * z - 8) % COLS, 1)
            high = pltpu.roll(edge[k], (COLS - 4 - GROUP * z) % COLS, 1)
            out.append(jnp.where(lane < 2, low, jnp.where(lane >= COLS - 2, high, inner[k, z])))
        new_lm[z] = out[0]
        new_mm[z] = out[1]
        coefficient[z] = jnp.maximum(out[0], 0.0) / out[1]


def f32(*shape):
    return jax.ShapeDtypeStruct(shape, jnp.float32)


def i32(*shape):
    return jax.ShapeDtypeStruct(shape, jnp.int32)


def kernel_call(kernel, outs, args, spaces=None, scratch=(), limit=16 * 1024):
    return pl.pallas_call(
        kernel,
        out_shape=outs,
        in_specs=[VMEM] * len(args) if spaces is None else spaces,
        out_specs=[VMEM] * len(outs),
        scratch_shapes=scratch,
        compiler_params=pltpu.CompilerParams(vmem_limit_bytes=limit * 1024),
    )(*args)


def even_pairs(count):
    return [(i, i ^ 1) for i in range(count)]


def odd_pairs(count):
    return [(i, (((i + 1) % count ^ 1) - 1) % count) for i in range(count)]


def body(velocity, old_lm, old_mm, offsets, fractions):
    nx, ny = lax.axis_size("gx"), lax.axis_size("gy")
    rows = 2 * PLANES + OLD
    held = [
        pltpu.VMEM((3, LEVELS, ROWS, COLS), jnp.float32),
        pltpu.VMEM((2, LEVELS, ROWS, COLS), jnp.float32),
    ]
    msg_a, msg_b = kernel_call(
        pack_kernel,
        [f32(rows, COLS), f32(rows, COLS)],
        (velocity, old_lm, old_mm),
        spaces=[HBM] * 3,
        scratch=held + [pltpu.SemaphoreType.DMA((3,))],
        limit=55190,
    )
    got_a = lax.ppermute(msg_a, "gy", even_pairs(ny))
    got_b = lax.ppermute(msg_b, "gy", odd_pairs(ny))
    tile = (ROWS, COLS)
    offsets, fractions, own_edges, near, near_off, near_frac = kernel_call(
        hold_kernel,
        [
            i32(3, LEVELS, *tile), f32(3, LEVELS, *tile), f32(*tile),
            f32(FIELDS, *tile), i32(3, *tile), f32(3, *tile),
        ],
        (offsets, fractions, velocity, old_lm, old_mm, msg_b),
        spaces=[HBM] * 5 + [VMEM],
        scratch=held + [pltpu.SemaphoreType.DMA((5,))],
        limit=55030,
    )
    outer, edges = kernel_call(
        rows_kernel, [f32(PLANES + OLD, *tile), f32(2 * ROWS, COLS)], (got_a, got_b, own_edges)
    )
    from_left = lax.ppermute(edges, "gx", [(i, (i + 1) % nx) for i in range(nx)])
    from_right = lax.ppermute(edges, "gx", [((i + 1) % nx, i) for i in range(nx)])
    inner, near_rows = kernel_call(
        inner_kernel,
        [f32(2, LEVELS, *tile), f32(FIELDS, *tile)],
        (velocity, old_lm, old_mm, offsets, fractions, outer),
    )
    out = f32(LEVELS, *tile)
    return tuple(
        kernel_call(
            edge_kernel,
            [out, out, out],
            (inner, near, near_rows, near_off, near_frac, from_right, from_left),
        )
    )


def solution(mesh):
    placed = (
        P(None, None, "gy", "gx"),
        P(None, "gy", "gx"),
        P(None, "gy", "gx"),
        P(None, None, "gy", "gx"),
        P(None, None, "gy", "gx"),
    )
    return jax.shard_map(
        body,
        mesh=mesh,
        in_specs=placed,
        out_specs=(P(None, "gy", "gx"), P(None, "gy", "gx"), P(None, "gy", "gx")),
        check_vma=False,
    )
```

time: 17.6 us -> 17.3 us (0.983)
  waiting for transfers between devices: 3.18 us -> 2.5 us
  Pallas kernels: 3.17 us -> 3.46 us
    ppermute x1, waiting for transfers between devices: 2.5 us -> 1.37 us  [body(): got_b = lax.ppermute(msg_b, 'gy', odd_pairs(ny))]
    ppermute x1, waiting for transfers between devices: 0.68 us -> 1.12 us  [body(): lax.ppermute(edges, 'gx', [(i, (i + 1) % nx) for i in range(nx)])]
    pallas_call x4 -> x5, Pallas kernels: 3.17 us -> 3.46 us  [kernel_call(): pl.pallas_call(kernel, out_shape=outs, in_specs=[VMEM] * len(args) if spa...]
  transfers between devices with their start and end apart: 4 -> 4, of which waited for: 2 -> 2; matrix products, arithmetic and copies ran while one was open for 0% -> 0% of each run, Pallas kernels for 5% -> 9%
where the time goes in v4:
time: 17.3 us; the launch traced here: 17.1 us
  starting transfers between devices  10.4 us (60%)
  Pallas kernels  3.46 us (20%)
  waiting for transfers between devices  2.5 us (14%)
  between operations  0.7 us (4%)
    ppermute x1, starting transfers between devices, body(): lax.ppermute(edges, 'gx', [((i + 1) % nx, i) for i in range(nx)])  6.66 us
    pallas_call x5, Pallas kernels, kernel_call(): pl.pallas_call(kernel, out_shape=outs, in_specs=[VMEM] * len(args) if spa...  3.46 us
    ppermute x1, starting transfers between devices, body(): lax.ppermute(edges, 'gx', [(i, (i + 1) % nx) for i in range(nx)])  1.99 us
    ppermute x1, starting transfers between devices, body(): got_b = lax.ppermute(msg_b, 'gy', odd_pairs(ny))  1.65 us
    ppermute x1, waiting for transfers between devices, body(): got_b = lax.ppermute(msg_b, 'gy', odd_pairs(ny))  1.37 us
    ppermute x1, waiting for transfers between devices, body(): lax.ppermute(edges, 'gx', [(i, (i + 1) % nx) for i in range(nx)])  1.12 us
  transfers between devices with their start and end apart: 4, of which 2 were waited for; matrix products, arithmetic and copies ran while one was open for 0% of the time, Pallas kernels for 9%

profile of v4, /device:TPU:2, one launch (start us, length us, event | category | flops | bytes accessed | tf_op | source)
XLA Modules:
  0.0 17.1 jit_solution(166417615564454638)
XLA Ops:
  0.6 0.0 copy-start.2
  0.6 0.0 copy-start.1
  0.7 0.9 %shard_map.76 = (f32[32,128]{1,0:T(8,128)S(1)}, f32[32,128]{1,0:T(8,128)S(1)}) custom-call(f32[3,4,8,128]{3,2,1,0:T(8,128)} %vel.1, f32[4,8,128]{2,1,0:T(8,128)} %old_lm.1, f32[4,8,128]{2,1,0:T(8,128)} %old_mm.1), custom_call_target="tpu_custom_call" | custom-call | tf_op jit(solution)/shard_map/pallas_call | solution.py:323
  1.5 0.1 collective-permute-start
  1.6 1.6 %collective-permute-start.1 = (f32[32,128]{1,0:T(8,128)S(1)}, f32[32,128]{1,0:T(8,128)S(1)}, u32[]{:S(2)}, u32[]{:S(2)}) collective-permute-start(f32[32,128]{1,0:T(8,128)S(1)} %get-tuple-element.15._), channel_id=1, source_target_pairs={{0,15},{1,2},{2,1},{3,4},{4,3},{5,6},{6,5},{7,8},{8,7},{9,10},{10,... | collective-permute-start | bytes 49160 | tf_op jit(solution)/shard_map/ppermute | solution.py:357
  3.3 0.0 copy-done.2
  3.3 0.0 copy-done.1
  3.3 0.0 copy-start
  3.3 1.1 %shard_map.77 = (s32[3,4,8,128]{3,2,1,0:T(8,128)S(1)}, f32[3,4,8,128]{3,2,1,0:T(8,128)S(1)}, f32[8,128]{1,0:T(8,128)S(1)}, f32[5,8,128]{2,1,0:T(8,128)S(1)}, s32...) custom-call(s32[3,4,8,128]{3,2,1,0:T(8,128)} %off_hbm.1, f32[3,4,8,128]{3,2,1,0:T(8,128)} %frac_hbm.1, ...), custom_call_target="tpu_custom_call" | custom-call | tf_op jit(solution)/shard_map/pallas_call | solution.py:323
  4.4 0.0 collective-permute-done.got_a
  4.4 1.4 %collective-permute-done.1.got_b = f32[32,128]{1,0:T(8,128)S(1)} collective-permute-done((f32[32,128]{1,0:T(8,128)S(1)}, f32[32,128]{1,0:T(8,128)S(1)}, u32[]{:S(2)}, u32[]{:S(2)}) %collective-permute-start.1) | collective-permute-done | bytes 16416 | tf_op jit(solution)/shard_map/ppermute | solution.py:357
  5.8 0.1 shard_map.78
  5.9 2.0 %collective-permute-start.3 = (f32[16,128]{1,0:T(8,128)S(1)}, f32[16,128]{1,0:T(8,128)S(1)}, u32[]{:S(2)}, u32[]{:S(2)}) collective-permute-start(f32[16,128]{1,0:T(8,128)S(1)} %get-tuple-element.26), channel_id=1, source_target_pairs={{0,16},{16,32},{32,48},{48,64},{64,80},{80,96},{96,112},{112,128},... | collective-permute-start | bytes 24584 | tf_op jit(solution)/shard_map/ppermute | solution.py:373
  7.9 6.7 %collective-permute-start.2 = (f32[16,128]{1,0:T(8,128)S(1)}, f32[16,128]{1,0:T(8,128)S(1)}, u32[]{:S(2)}, u32[]{:S(2)}) collective-permute-start(f32[16,128]{1,0:T(8,128)S(1)} %get-tuple-element.26), channel_id=1, source_target_pairs={{16,0},{32,16},{48,32},{64,48},{80,64},{96,80},{112,96},{128,112},... | collective-permute-start | bytes 24584 | tf_op jit(solution)/shard_map/ppermute | solution.py:374
  14.5 0.0 copy-done
  14.5 0.4 %shard_map.79 = (f32[2,4,8,128]{3,2,1,0:T(8,128)S(1)}, f32[5,8,128]{2,1,0:T(8,128)S(1)}) custom-call(f32[3,4,8,128]{3,2,1,0:T(8,128)S(1)} %copy-done, f32[4,8,128]{2,1,0:T(8,128)S(1)} %copy-done.1, f32[4,8,128]{2,1,0:T(8,128)S(1)} %copy-done.2, s32[3,4,8,128]{3,2,1,0:T(8,128)S(1)} %get-tuple-element.16.offsets, ...), custom_call_target="tpu_custom_call" | custom-call | tf_op jit(solution)/shard_map/pallas_call | solution.py:323
  14.9 1.1 %collective-permute-done.3.from_left = f32[16,128]{1,0:T(8,128)S(1)} collective-permute-done((f32[16,128]{1,0:T(8,128)S(1)}, f32[16,128]{1,0:T(8,128)S(1)}, u32[]{:S(2)}, u32[]{:S(2)}) %collective-permute-start.3) | collective-permute-done | bytes 8224 | tf_op jit(solution)/shard_map/ppermute | solution.py:373
  16.1 0.0 collective-permute-done.2.from_right
  16.1 1.0 %shard_map.80 = (f32[4,8,128]{2,1,0:T(8,128)}, f32[4,8,128]{2,1,0:T(8,128)}, f32[4,8,128]{2,1,0:T(8,128)}) custom-call(f32[2,4,8,128]{3,2,1,0:T(8,128)S(1)} %get-tuple-element.21.inner, f32[5,8,128]{2,1,0:T(8,128)S(1)} %get-tuple-element.22.near, f32[5,8,128]{2,1,0:T(8,128)S(1)} %get-tuple-element.23.near_rows, s32[3,8,128]{2,1,0:T(8,128)S(1)} %get-tuple-element.24.near_off, ...), custom_call_target="tpu_custom_call" | custom-call | tf_op jit(solution)/shard_map/pallas_call | solution.py:323
Async XLA Ops:
  0.6 2.6 %copy-start.2 = (f32[4,8,128]{2,1,0:T(8,128)S(1)}, f32[4,8,128]{2,1,0:T(8,128)}, u32[]{:S(2)}) copy-start(f32[4,8,128]{2,1,0:T(8,128)} %old_mm.1) | copy-start | bytes 49156
  0.6 2.6 %copy-start.1 = (f32[4,8,128]{2,1,0:T(8,128)S(1)}, f32[4,8,128]{2,1,0:T(8,128)}, u32[]{:S(2)}) copy-start(f32[4,8,128]{2,1,0:T(8,128)} %old_lm.1) | copy-start | bytes 49156
  1.5 2.9 %collective-permute-start = (f32[32,128]{1,0:T(8,128)S(1)}, f32[32,128]{1,0:T(8,128)S(1)}, u32[]{:S(2)}, u32[]{:S(2)}) collective-permute-start(f32[32,128]{1,0:T(8,128)S(1)} %get-tuple-element.18), channel_id=1, source_target_pairs={{0,1},{1,0},{2,3},{3,2},{4,5},{5,4},{6,7},{7,6},{8,9},{9,8},{10,11... | collective-permute-start | bytes 49160 | tf_op jit(solution)/shard_map/ppermute | solution.py:356
  1.6 4.2 %collective-permute-start.1 = (f32[32,128]{1,0:T(8,128)S(1)}, f32[32,128]{1,0:T(8,128)S(1)}, u32[]{:S(2)}, u32[]{:S(2)}) collective-permute-start(f32[32,128]{1,0:T(8,128)S(1)} %get-tuple-element.15._), channel_id=1, source_target_pairs={{0,15},{1,2},{2,1},{3,4},{4,3},{5,6},{6,5},{7,8},{8,7},{9,10},{10,... | collective-permute-start | bytes 49160 | tf_op jit(solution)/shard_map/ppermute | solution.py:357
  3.3 11.3 %copy-start = (f32[3,4,8,128]{3,2,1,0:T(8,128)S(1)}, f32[3,4,8,128]{3,2,1,0:T(8,128)}, u32[]{:S(2)}) copy-start(f32[3,4,8,128]{3,2,1,0:T(8,128)} %vel.1) | copy-start | bytes 147460
  5.9 10.2 %collective-permute-start.3 = (f32[16,128]{1,0:T(8,128)S(1)}, f32[16,128]{1,0:T(8,128)S(1)}, u32[]{:S(2)}, u32[]{:S(2)}) collective-permute-start(f32[16,128]{1,0:T(8,128)S(1)} %get-tuple-element.26), channel_id=1, source_target_pairs={{0,16},{16,32},{32,48},{48,64},{64,80},{80,96},{96,112},{112,128},... | collective-permute-start | bytes 24584 | tf_op jit(solution)/shard_map/ppermute | solution.py:373
  7.9 8.2 %collective-permute-start.2 = (f32[16,128]{1,0:T(8,128)S(1)}, f32[16,128]{1,0:T(8,128)S(1)}, u32[]{:S(2)}, u32[]{:S(2)}) collective-permute-start(f32[16,128]{1,0:T(8,128)S(1)} %get-tuple-element.26), channel_id=1, source_target_pairs={{16,0},{32,16},{48,32},{64,48},{80,64},{96,80},{112,96},{128,112},... | collective-permute-start | bytes 24584 | tf_op jit(solution)/shard_map/ppermute | solution.py:374

commit v5 on v4

--- a/solution.py
+++ b/solution.py
@@ -72,34 +72,7 @@
         msg_b[at : at + 1, :] = ref[pl.ds(7 - 7 * even, 1), :]
 
 
-def hold_kernel(
-    off_hbm, frac_hbm, vel_hbm, lm_hbm, mm_hbm, _,
-    off, frac, edges, near, near_off, near_frac, vel, old, sems,
-):
-    pairs = (
-        (vel_hbm, vel), (lm_hbm, old.at[0]), (mm_hbm, old.at[1]), (off_hbm, off), (frac_hbm, frac)
-    )
-    copies = [pltpu.make_async_copy(*pair, sems.at[k]) for k, pair in enumerate(pairs)]
-    for copy in copies:
-        copy.start()
-    for copy in copies:
-        copy.wait()
-
-    def tile(field, z):
-        return vel[field, z] if field < 3 else old[field - 3, z]
-
-    edges[...] = packed_edges(tile)
-    for field in range(FIELDS):
-        near[field] = edge_domain(lambda z: tile(field, z))
-    for k in range(3):
-        near_off[k] = edge_domain(lambda z: off[k, z])
-        near_frac[k] = edge_domain(lambda z: frac[k, z])
-
-
-def rows_kernel(got_a, got_b, own_edges, outer, edges):
-    even = lax.axis_index("gy") % 2 == 0
-    above = jnp.where(even, got_a[...], got_b[...])
-    below = jnp.where(even, got_b[...], got_a[...])
+def fill_outer(above, below, outer):
     outer[...] = jnp.zeros_like(outer)
     for plane in range(PLANES):
         outer[plane, 0:2, :] = above[2 * plane : 2 * plane + 2]
@@ -107,6 +80,25 @@
     for plane in range(PLANES, PLANES + OLD):
         outer[plane, 0:1, :] = above[PLANES + plane : PLANES + plane + 1]
         outer[plane, 7:8, :] = below[PLANES + plane : PLANES + plane + 1]
+
+
+def first_edges_kernel(got_a, vel, old_lm, old_mm, own_edges, edges, wide, outer):
+    def tile(field, z):
+        return vel[field, z] if field < 3 else (old_lm, old_mm)[field - 3][z]
+
+    own_edges[...] = packed_edges(tile)
+    wide[0:ROWS, :] = own_edges[...]
+    wide[ROWS:, :] = jnp.zeros_like(wide[ROWS:, :])
+    fill_outer(got_a[...], got_a[...], outer)
+    edges[0:ROWS, :] = own_edges[...]
+    edges[ROWS:, :] = packed_edges(lambda field, z: outer[LEVELS * field + z])
+
+
+def rows_kernel(got_a, got_b, own_edges, outer, edges):
+    even = lax.axis_index("gy") % 2 == 0
+    above = jnp.where(even, got_a[...], got_b[...])
+    below = jnp.where(even, got_b[...], got_a[...])
+    fill_outer(above, below, outer)
     edges[0:ROWS, :] = own_edges[...]
     edges[ROWS:, :] = packed_edges(lambda field, z: outer[LEVELS * field + z])
 
@@ -273,24 +265,34 @@
     return results
 
 
-def inner_kernel(vel, old_lm, old_mm, offsets, fractions, outer, new, near_rows):
+def inner_kernel(
+    vel, old_lm, old_mm, offsets, fractions, outer, new, near, near_rows, near_off, near_frac
+):
     fields = [vel[c] for c in range(3)] + [old_lm[...], old_mm[...]]
     fields = [(own, outer[LEVELS * f : LEVELS * (f + 1)]) for f, own in enumerate(fields)]
     new[0], new[1] = update(Grid(), fields, [offsets[k] for k in range(3)], [fractions[k] for k in range(3)])
-    for field in range(FIELDS):
-        near_rows[field] = edge_domain(lambda z: outer[LEVELS * field + z])
+    for field, (own, rows) in enumerate(fields):
+        near[field] = edge_domain(lambda z: own[z])
+        near_rows[field] = edge_domain(lambda z: rows[z])
+    for k in range(3):
+        near_off[k] = edge_domain(lambda z: offsets[k, z])
+        near_frac[k] = edge_domain(lambda z: fractions[k, z])
 
 
 def edge_kernel(
-    inner, near, near_rows, near_off, near_frac, from_right, from_left, new_lm, new_mm, coefficient
+    inner, near, near_rows, near_off, near_frac, from_right, left_a, left_b, new_lm, new_mm, coefficient
 ):
     right = from_right_mask()
     place = lanes() % GROUP
     is_right, is_left = (place == 4) | (place == 5), (place == 6) | (place == 7)
+    even = lax.axis_index("gy") % 2 == 0
+    upper = lax.broadcasted_iota(jnp.int32, (ROWS, COLS), 0) < ROWS // 2
+    first, second = left_a[ROWS:, :], left_b[0:ROWS, :]
+    corners = jnp.where(even, jnp.where(upper, first, second), jnp.where(upper, second, first))
+    from_left = (left_a[0:ROWS, :], corners)
     pairs = [[], []]
     for half, own in enumerate((near, near_rows)):
-        at = slice(half * ROWS, (half + 1) * ROWS)
-        halo = jnp.where(right, from_right[at, :], from_left[at, :])
+        halo = jnp.where(right, from_right[half * ROWS : (half + 1) * ROWS, :], from_left[half])
         for field in range(FIELDS):
             first = 4 * field if field < 3 else 12 + 2 * (field - 3)
             to_right = (4 - first - (2 if field < 3 else 1)) % COLS
@@ -356,25 +358,24 @@
     got_a = lax.ppermute(msg_a, "gy", even_pairs(ny))
     got_b = lax.ppermute(msg_b, "gy", odd_pairs(ny))
     tile = (ROWS, COLS)
-    offsets, fractions, own_edges, near, near_off, near_frac = kernel_call(
-        hold_kernel,
-        [
-            i32(3, LEVELS, *tile), f32(3, LEVELS, *tile), f32(*tile),
-            f32(FIELDS, *tile), i32(3, *tile), f32(3, *tile),
-        ],
-        (offsets, fractions, velocity, old_lm, old_mm, msg_b),
-        spaces=[HBM] * 5 + [VMEM],
-        scratch=held + [pltpu.SemaphoreType.DMA((5,))],
-        limit=55030,
+    own_edges, edges, wide = kernel_call(
+        first_edges_kernel,
+        [f32(*tile), f32(2 * ROWS, COLS), f32(3 * ROWS, COLS)],
+        (got_a, velocity, old_lm, old_mm),
+        scratch=[pltpu.VMEM((PLANES + OLD, *tile), jnp.float32)],
+    )
+    to_east = [(i, (i + 1) % nx) for i in range(nx)]
+    left_a = lax.ppermute(edges, "gx", to_east)
+    left_b = lax.ppermute(
+        wide, ("gx", "gy"), [(i * ny + j, k * ny + m) for i, k in to_east for j, m in odd_pairs(ny)]
     )
     outer, edges = kernel_call(
         rows_kernel, [f32(PLANES + OLD, *tile), f32(2 * ROWS, COLS)], (got_a, got_b, own_edges)
     )
-    from_left = lax.ppermute(edges, "gx", [(i, (i + 1) % nx) for i in range(nx)])
-    from_right = lax.ppermute(edges, "gx", [((i + 1) % nx, i) for i in range(nx)])
-    inner, near_rows = kernel_call(
+    from_right = lax.ppermute(edges, "gx", [(k, i) for i, k in to_east])
+    inner, near, near_rows, near_off, near_frac = kernel_call(
         inner_kernel,
-        [f32(2, LEVELS, *tile), f32(FIELDS, *tile)],
+        [f32(2, LEVELS, *tile), f32(FIELDS, *tile), f32(FIELDS, *tile), i32(3, *tile), f32(3, *tile)],
         (velocity, old_lm, old_mm, offsets, fractions, outer),
     )
     out = f32(LEVELS, *tile)
@@ -382,7 +383,7 @@
         kernel_call(
             edge_kernel,
             [out, out, out],
-            (inner, near, near_rows, near_off, near_frac, from_right, from_left),
+            (inner, near, near_rows, near_off, near_frac, from_right, left_a, left_b),
         )
     )
 

time: 17.3 us -> 17 us (0.983)
  starting transfers between devices: 10.4 us -> 12.7 us
  waiting for transfers between devices: 2.5 us -> 0.85 us
  Pallas kernels: 3.46 us -> 2.63 us
    ppermute x2 -> x3, starting transfers between devices: 8.65 us -> 10.9 us  [the longest x1 6.48 us: body(): from_right = lax.ppermute(edges, 'gx', [(k, i) for i, k in to_east])]
    ppermute x1, waiting for transfers between devices: 1.37 us -> 0.01 us  [body(): got_b = lax.ppermute(msg_b, 'gy', odd_pairs(ny))]
    pallas_call x5, Pallas kernels: 3.46 us -> 2.63 us  [kernel_call(): pl.pallas_call(kernel, out_shape=outs, in_specs=[VMEM] * len(args) if spa...]
    ppermute x2 -> x3, waiting for transfers between devices: 1.12 us -> 0.84 us  [the longest x1 0.84 us: body(): from_right = lax.ppermute(edges, 'gx', [(k, i) for i, k in to_east])]
  transfers between devices with their start and end apart: 4 -> 5, of which waited for: 2 -> 1; matrix products, arithmetic and copies ran while one was open for 0% -> 0% of each run, Pallas kernels for 9% -> 4%
where the time goes in v5:
time: 17 us; the launch traced here: 16.9 us
  starting transfers between devices  12.7 us (75%)
  Pallas kernels  2.63 us (15%)
  waiting for transfers between devices  0.85 us (5%)
  between operations  0.73 us (4%)
    ppermute x1, starting transfers between devices, body(): from_right = lax.ppermute(edges, 'gx', [(k, i) for i, k in to_east])  6.48 us
    pallas_call x5, Pallas kernels, kernel_call(): pl.pallas_call(kernel, out_shape=outs, in_specs=[VMEM] * len(args) if spa...  2.63 us
    ppermute x1, starting transfers between devices, body(): lax.ppermute(wide, ('gx', 'gy'), [(i * ny + j, k * ny + m) for i, k in to...  2.53 us
    ppermute x1, starting transfers between devices, body(): left_a = lax.ppermute(edges, 'gx', to_east)  1.92 us
    ppermute x1, starting transfers between devices, body(): got_b = lax.ppermute(msg_b, 'gy', odd_pairs(ny))  1.63 us
    ppermute x1, waiting for transfers between devices, body(): from_right = lax.ppermute(edges, 'gx', [(k, i) for i, k in to_east])  0.84 us
  transfers between devices with their start and end apart: 5, of which 1 were waited for; matrix products, arithmetic and copies ran while one was open for 0% of the time, Pallas kernels for 4%

profile of v5, /device:TPU:2, one launch (start us, length us, event | category | flops | bytes accessed | tf_op | source)
XLA Modules:
  0.0 16.9 jit_solution(14766127246080975531)
XLA Ops:
  0.6 0.0 copy-start.2
  0.6 0.0 copy-start.1
  0.7 0.0 copy-start
  0.7 0.9 %shard_map.76 = (f32[32,128]{1,0:T(8,128)S(1)}, f32[32,128]{1,0:T(8,128)S(1)}) custom-call(f32[3,4,8,128]{3,2,1,0:T(8,128)} %vel.3, f32[4,8,128]{2,1,0:T(8,128)} %old_lm.3, f32[4,8,128]{2,1,0:T(8,128)} %old_mm.3), custom_call_target="tpu_custom_call" | custom-call | tf_op jit(solution)/shard_map/pallas_call | solution.py:325
  1.6 0.1 collective-permute-start
  1.7 0.0 copy-start.3
  1.7 0.0 copy-start.4
  1.7 1.6 %collective-permute-start.1 = (f32[32,128]{1,0:T(8,128)S(1)}, f32[32,128]{1,0:T(8,128)S(1)}, u32[]{:S(2)}, u32[]{:S(2)}) collective-permute-start(f32[32,128]{1,0:T(8,128)S(1)} %get-tuple-element.16), channel_id=1, source_target_pairs={{0,15},{1,2},{2,1},{3,4},{4,3},{5,6},{6,5},{7,8},{8,7},{9,10},{10,... | collective-permute-start | bytes 49160 | tf_op jit(solution)/shard_map/ppermute | solution.py:359
  3.3 0.0 collective-permute-done.got_a
  3.3 0.0 copy-done.2
  3.3 0.0 copy-done.1
  3.3 0.0 copy-done
  3.4 0.1 shard_map.77
  3.5 2.5 %collective-permute-start.4 = (f32[24,128]{1,0:T(8,128)S(1)}, f32[24,128]{1,0:T(8,128)S(1)}, u32[]{:S(2)}, u32[]{:S(2)}) collective-permute-start(f32[24,128]{1,0:T(8,128)S(1)} %get-tuple-element.26), channel_id=1, source_target_pairs={{0,31},{1,18},{2,17},{3,20},{4,19},{5,22},{6,21},{7,24},{8,23},{9,... | collective-permute-start | bytes 36872 | tf_op jit(solution)/shard_map/ppermute | solution.py:369
  6.0 1.9 %collective-permute-start.3 = (f32[16,128]{1,0:T(8,128)S(1)}, f32[16,128]{1,0:T(8,128)S(1)}, u32[]{:S(2)}, u32[]{:S(2)}) collective-permute-start(f32[16,128]{1,0:T(8,128)S(1)} %get-tuple-element.25), channel_id=1, source_target_pairs={{0,16},{16,32},{32,48},{48,64},{64,80},{80,96},{96,112},{112,128},... | collective-permute-start | bytes 24584 | tf_op jit(solution)/shard_map/ppermute | solution.py:368
  7.9 0.0 collective-permute-done.1.got_b
  7.9 0.1 shard_map.78
  8.0 6.5 %collective-permute-start.2 = (f32[16,128]{1,0:T(8,128)S(1)}, f32[16,128]{1,0:T(8,128)S(1)}, u32[]{:S(2)}, u32[]{:S(2)}) collective-permute-start(f32[16,128]{1,0:T(8,128)S(1)} %get-tuple-element.24), channel_id=1, source_target_pairs={{16,0},{32,16},{48,32},{64,48},{80,64},{96,80},{112,96},{128,112},... | collective-permute-start | bytes 24584 | tf_op jit(solution)/shard_map/ppermute | solution.py:375
  14.5 0.0 copy-done.4
  14.5 0.5 %shard_map.79 = (f32[2,4,8,128]{3,2,1,0:T(8,128)S(1)}, f32[5,8,128]{2,1,0:T(8,128)S(1)}, f32[5,8,128]{2,1,0:T(8,128)S(1)}, s32[3,8,128]{2,1,0:T(8,128)S(1)}, f32[3,8,128]{2,1,0:T(8,128)S(1)}) custom-call(f32[3,4,8,128]{3,2,1,0:T(8,128)S(1)} %copy-done, f32[4,8,128]{2,1,0:T(8,128)S(1)} %copy-done.1, f32[4,8,128]{2,1,0:T(8,128)S(1)} %copy-done.2, ...), custom_call_target="tpu_custom_call" | custom-call | tf_op jit(solution)/shard_map/pallas_call | solution.py:325
  15.0 0.0 collective-permute-done.3.left_a
  15.1 0.8 %collective-permute-done.2.from_right = f32[16,128]{1,0:T(8,128)S(1)} collective-permute-done((f32[16,128]{1,0:T(8,128)S(1)}, f32[16,128]{1,0:T(8,128)S(1)}, u32[]{:S(2)}, u32[]{:S(2)}) %collective-permute-start.2) | collective-permute-done | bytes 8224 | tf_op jit(solution)/shard_map/ppermute | solution.py:375
  15.9 0.0 collective-permute-done.4.left_b
  15.9 1.0 %shard_map.80 = (f32[4,8,128]{2,1,0:T(8,128)}, f32[4,8,128]{2,1,0:T(8,128)}, f32[4,8,128]{2,1,0:T(8,128)}) custom-call(f32[2,4,8,128]{3,2,1,0:T(8,128)S(1)} %get-tuple-element.19.inner, f32[5,8,128]{2,1,0:T(8,128)S(1)} %get-tuple-element.20.near, f32[5,8,128]{2,1,0:T(8,128)S(1)} %get-tuple-element.21.near_rows, s32[3,8,128]{2,1,0:T(8,128)S(1)} %get-tuple-element.22.near_off, ...), custom_call_target="tpu_custom_call" | custom-call | tf_op jit(solution)/shard_map/pallas_call | solution.py:325
  (1 shorter events, 0.0 us)
Async XLA Ops:
  0.6 2.7 %copy-start.2 = (f32[4,8,128]{2,1,0:T(8,128)S(1)}, f32[4,8,128]{2,1,0:T(8,128)}, u32[]{:S(2)}) copy-start(f32[4,8,128]{2,1,0:T(8,128)} %old_mm.3) | copy-start | bytes 49156
  0.6 2.7 %copy-start.1 = (f32[4,8,128]{2,1,0:T(8,128)S(1)}, f32[4,8,128]{2,1,0:T(8,128)}, u32[]{:S(2)}) copy-start(f32[4,8,128]{2,1,0:T(8,128)} %old_lm.3) | copy-start | bytes 49156
  0.7 2.7 %copy-start = (f32[3,4,8,128]{3,2,1,0:T(8,128)S(1)}, f32[3,4,8,128]{3,2,1,0:T(8,128)}, u32[]{:S(2)}) copy-start(f32[3,4,8,128]{3,2,1,0:T(8,128)} %vel.3) | copy-start | bytes 147460
  1.6 1.8 %collective-permute-start = (f32[32,128]{1,0:T(8,128)S(1)}, f32[32,128]{1,0:T(8,128)S(1)}, u32[]{:S(2)}, u32[]{:S(2)}) collective-permute-start(f32[32,128]{1,0:T(8,128)S(1)} %get-tuple-element.15), channel_id=1, source_target_pairs={{0,1},{1,0},{2,3},{3,2},{4,5},{5,4},{6,7},{7,6},{8,9},{9,8},{10,11... | collective-permute-start | bytes 49160 | tf_op jit(solution)/shard_map/ppermute | solution.py:358
  1.7 12.8 %copy-start.3 = (s32[3,4,8,128]{3,2,1,0:T(8,128)S(1)}, s32[3,4,8,128]{3,2,1,0:T(8,128)}, u32[]{:S(2)}) copy-start(s32[3,4,8,128]{3,2,1,0:T(8,128)} %offsets.1) | copy-start | bytes 147460
  1.7 12.8 %copy-start.4 = (f32[3,4,8,128]{3,2,1,0:T(8,128)S(1)}, f32[3,4,8,128]{3,2,1,0:T(8,128)}, u32[]{:S(2)}) copy-start(f32[3,4,8,128]{3,2,1,0:T(8,128)} %fractions.1) | copy-start | bytes 147460
  1.7 6.2 %collective-permute-start.1 = (f32[32,128]{1,0:T(8,128)S(1)}, f32[32,128]{1,0:T(8,128)S(1)}, u32[]{:S(2)}, u32[]{:S(2)}) collective-permute-start(f32[32,128]{1,0:T(8,128)S(1)} %get-tuple-element.16), channel_id=1, source_target_pairs={{0,15},{1,2},{2,1},{3,4},{4,3},{5,6},{6,5},{7,8},{8,7},{9,10},{10,... | collective-permute-start | bytes 49160 | tf_op jit(solution)/shard_map/ppermute | solution.py:359
  3.5 12.4 %collective-permute-start.4 = (f32[24,128]{1,0:T(8,128)S(1)}, f32[24,128]{1,0:T(8,128)S(1)}, u32[]{:S(2)}, u32[]{:S(2)}) collective-permute-start(f32[24,128]{1,0:T(8,128)S(1)} %get-tuple-element.26), channel_id=1, source_target_pairs={{0,31},{1,18},{2,17},{3,20},{4,19},{5,22},{6,21},{7,24},{8,23},{9,... | collective-permute-start | bytes 36872 | tf_op jit(solution)/shard_map/ppermute | solution.py:369
  6.0 9.0 %collective-permute-start.3 = (f32[16,128]{1,0:T(8,128)S(1)}, f32[16,128]{1,0:T(8,128)S(1)}, u32[]{:S(2)}, u32[]{:S(2)}) collective-permute-start(f32[16,128]{1,0:T(8,128)S(1)} %get-tuple-element.25), channel_id=1, source_target_pairs={{0,16},{16,32},{32,48},{48,64},{64,80},{80,96},{96,112},{112,128},... | collective-permute-start | bytes 24584 | tf_op jit(solution)/shard_map/ppermute | solution.py:368
  8.0 7.8 %collective-permute-start.2 = (f32[16,128]{1,0:T(8,128)S(1)}, f32[16,128]{1,0:T(8,128)S(1)}, u32[]{:S(2)}, u32[]{:S(2)}) collective-permute-start(f32[16,128]{1,0:T(8,128)S(1)} %get-tuple-element.24), channel_id=1, source_target_pairs={{16,0},{32,16},{48,32},{64,48},{80,64},{96,80},{112,96},{128,112},... | collective-permute-start | bytes 24584 | tf_op jit(solution)/shard_map/ppermute | solution.py:375

commit v6 on v5

--- a/solution.py
+++ b/solution.py
@@ -16,6 +16,7 @@
 FIELDS = 5
 PLANES = 3 * LEVELS
 OLD = 2 * LEVELS
+HALF = COLS // 2
 GROUP = 16
 VMEM = pl.BlockSpec(memory_space=pltpu.VMEM)
 HBM = pl.BlockSpec(memory_space=pltpu.HBM)
@@ -25,20 +26,15 @@
     return lax.broadcasted_iota(jnp.int32, (ROWS, COLS), 1)
 
 
-def packed_edges(tile):
+def packed_edges(tile, base=0):
     lane = lanes()
     packed = None
     for z in range(LEVELS):
         for field in range(FIELDS):
-            first = GROUP * z + (4 * field if field < 3 else 12 + 2 * (field - 3))
+            first = base + GROUP * z + (4 * field if field < 3 else 12 + 2 * (field - 3))
             moved = pltpu.roll(tile(field, z), first + (2 if field < 3 else 1), 1)
             packed = moved if packed is None else jnp.where(lane >= first, moved, packed)
     return packed
-
-
-def from_right_mask():
-    lane = lanes() % GROUP
-    return jnp.where(lane < 12, lane % 4, 2 * (lane % 2)) >= 2
 
 
 def edge_domain(tile):
@@ -90,8 +86,8 @@
     wide[0:ROWS, :] = own_edges[...]
     wide[ROWS:, :] = jnp.zeros_like(wide[ROWS:, :])
     fill_outer(got_a[...], got_a[...], outer)
-    edges[0:ROWS, :] = own_edges[...]
-    edges[ROWS:, :] = packed_edges(lambda field, z: outer[LEVELS * field + z])
+    rows = packed_edges(lambda field, z: outer[LEVELS * field + z], HALF)
+    edges[...] = jnp.where(lanes() < HALF, own_edges[...], rows)
 
 
 def rows_kernel(got_a, got_b, own_edges, outer, edges):
@@ -99,8 +95,8 @@
     above = jnp.where(even, got_a[...], got_b[...])
     below = jnp.where(even, got_b[...], got_a[...])
     fill_outer(above, below, outer)
-    edges[0:ROWS, :] = own_edges[...]
-    edges[ROWS:, :] = packed_edges(lambda field, z: outer[LEVELS * field + z])
+    rows = packed_edges(lambda field, z: outer[LEVELS * field + z], HALF)
+    edges[...] = jnp.where(lanes() < HALF, own_edges[...], rows)
 
 
 class Grid:
@@ -282,23 +278,24 @@
 def edge_kernel(
     inner, near, near_rows, near_off, near_frac, from_right, left_a, left_b, new_lm, new_mm, coefficient
 ):
-    right = from_right_mask()
     place = lanes() % GROUP
     is_right, is_left = (place == 4) | (place == 5), (place == 6) | (place == 7)
     even = lax.axis_index("gy") % 2 == 0
     upper = lax.broadcasted_iota(jnp.int32, (ROWS, COLS), 0) < ROWS // 2
-    first, second = left_a[ROWS:, :], left_b[0:ROWS, :]
-    corners = jnp.where(even, jnp.where(upper, first, second), jnp.where(upper, second, first))
-    from_left = (left_a[0:ROWS, :], corners)
+    east = from_right[...]
+    first, second = left_a[...], pltpu.roll(left_b[0:ROWS, :], HALF, 1)
+    west = (
+        first,
+        jnp.where(even, jnp.where(upper, first, second), jnp.where(upper, second, first)),
+    )
     pairs = [[], []]
     for half, own in enumerate((near, near_rows)):
-        halo = jnp.where(right, from_right[half * ROWS : (half + 1) * ROWS, :], from_left[half])
         for field in range(FIELDS):
-            first = 4 * field if field < 3 else 12 + 2 * (field - 3)
-            to_right = (4 - first - (2 if field < 3 else 1)) % COLS
-            to_left = ((6 if field < 3 else 7) - first) % COLS
-            tile = jnp.where(is_left, pltpu.roll(halo, to_left, 1), own[field])
-            pairs[half].append(jnp.where(is_right, pltpu.roll(halo, to_right, 1), tile))
+            at = HALF * half + (4 * field if field < 3 else 12 + 2 * (field - 3))
+            to_right = (4 - at - (2 if field < 3 else 1)) % COLS
+            to_left = ((6 if field < 3 else 7) - at) % COLS
+            tile = jnp.where(is_left, pltpu.roll(west[half], to_left, 1), own[field])
+            pairs[half].append(jnp.where(is_right, pltpu.roll(east, to_right, 1), tile))
     fields = list(zip(*pairs))
     edge = update(EdgeGrid(), fields, [near_off[k] for k in range(3)], [near_frac[k] for k in range(3)])
     lane = lanes()
@@ -360,7 +357,7 @@
     tile = (ROWS, COLS)
     own_edges, edges, wide = kernel_call(
         first_edges_kernel,
-        [f32(*tile), f32(2 * ROWS, COLS), f32(3 * ROWS, COLS)],
+        [f32(*tile), f32(*tile), f32(2 * ROWS, COLS)],
         (got_a, velocity, old_lm, old_mm),
         scratch=[pltpu.VMEM((PLANES + OLD, *tile), jnp.float32)],
     )
@@ -370,7 +367,7 @@
         wide, ("gx", "gy"), [(i * ny + j, k * ny + m) for i, k in to_east for j, m in odd_pairs(ny)]
     )
     outer, edges = kernel_call(
-        rows_kernel, [f32(PLANES + OLD, *tile), f32(2 * ROWS, COLS)], (got_a, got_b, own_edges)
+        rows_kernel, [f32(PLANES + OLD, *tile), f32(*tile)], (got_a, got_b, own_edges)
     )
     from_right = lax.ppermute(edges, "gx", [(k, i) for i, k in to_east])
     inner, near, near_rows, near_off, near_frac = kernel_call(

time: 17 us -> 17.1 us (level)
  no operation moved by 1% of the time
where the time goes in v6:
time: 17.1 us; the launch traced here: 16.9 us
  starting transfers between devices  12.7 us (74%)
  Pallas kernels  2.72 us (16%)
  waiting for transfers between devices  0.81 us (5%)
  between operations  0.73 us (4%)
    ppermute x1, starting transfers between devices, body(): from_right = lax.ppermute(edges, 'gx', [(k, i) for i, k in to_east])  6.48 us
    pallas_call x5, Pallas kernels, kernel_call(): pl.pallas_call(kernel, out_shape=outs, in_specs=[VMEM] * len(args) if spa...  2.72 us
    ppermute x1, starting transfers between devices, body(): lax.ppermute(wide, ('gx', 'gy'), [(i * ny + j, k * ny + m) for i, k in to...  2.53 us
    ppermute x1, starting transfers between devices, body(): left_a = lax.ppermute(edges, 'gx', to_east)  1.92 us
    ppermute x1, starting transfers between devices, body(): got_b = lax.ppermute(msg_b, 'gy', odd_pairs(ny))  1.63 us
    ppermute x1, waiting for transfers between devices, body(): from_right = lax.ppermute(edges, 'gx', [(k, i) for i, k in to_east])  0.8 us
  transfers between devices with their start and end apart: 5, of which 1 were waited for; matrix products, arithmetic and copies ran while one was open for 0% of the time, Pallas kernels for 4%

profile of v6, /device:TPU:2, one launch (start us, length us, event | category | flops | bytes accessed | tf_op | source)
XLA Modules:
  0.0 16.9 jit_solution(14117467415658506391)
XLA Ops:
  0.6 0.0 copy-start.2
  0.6 0.0 copy-start.1
  0.7 0.0 copy-start
  0.7 0.9 %shard_map.76 = (f32[32,128]{1,0:T(8,128)S(1)}, f32[32,128]{1,0:T(8,128)S(1)}) custom-call(f32[3,4,8,128]{3,2,1,0:T(8,128)} %vel.3, f32[4,8,128]{2,1,0:T(8,128)} %old_lm.3, f32[4,8,128]{2,1,0:T(8,128)} %old_mm.3), custom_call_target="tpu_custom_call" | custom-call | tf_op jit(solution)/shard_map/pallas_call | solution.py:322
  1.6 0.1 collective-permute-start
  1.7 0.0 copy-start.3
  1.7 0.0 copy-start.4
  1.7 1.6 %collective-permute-start.1 = (f32[32,128]{1,0:T(8,128)S(1)}, f32[32,128]{1,0:T(8,128)S(1)}, u32[]{:S(2)}, u32[]{:S(2)}) collective-permute-start(f32[32,128]{1,0:T(8,128)S(1)} %get-tuple-element.16), channel_id=1, source_target_pairs={{0,15},{1,2},{2,1},{3,4},{4,3},{5,6},{6,5},{7,8},{8,7},{9,10},{10,... | collective-permute-start | bytes 49160 | tf_op jit(solution)/shard_map/ppermute | solution.py:356
  3.3 0.0 collective-permute-done.got_a
  3.3 0.0 copy-done.2
  3.3 0.0 copy-done.1
  3.3 0.0 copy-done
  3.4 0.1 shard_map.77
  3.5 2.5 %collective-permute-start.4 = (f32[16,128]{1,0:T(8,128)S(1)}, f32[16,128]{1,0:T(8,128)S(1)}, u32[]{:S(2)}, u32[]{:S(2)}) collective-permute-start(f32[16,128]{1,0:T(8,128)S(1)} %get-tuple-element.26), channel_id=1, source_target_pairs={{0,31},{1,18},{2,17},{3,20},{4,19},{5,22},{6,21},{7,24},{8,23},{9,... | collective-permute-start | bytes 24584 | tf_op jit(solution)/shard_map/ppermute | solution.py:366
  6.0 1.9 %collective-permute-start.3 = (f32[8,128]{1,0:T(8,128)S(1)}, f32[8,128]{1,0:T(8,128)S(1)}, u32[]{:S(2)}, u32[]{:S(2)}) collective-permute-start(f32[8,128]{1,0:T(8,128)S(1)} %get-tuple-element.25), channel_id=1, source_target_pairs={{0,16},{16,32},{32,48},{48,64},{64,80},{80,96},{96,112},{112,128},... | collective-permute-start | bytes 12296 | tf_op jit(solution)/shard_map/ppermute | solution.py:365
  7.9 0.0 collective-permute-done.1.got_b
  7.9 0.1 shard_map.78
  8.0 6.5 %collective-permute-start.2 = (f32[8,128]{1,0:T(8,128)S(1)}, f32[8,128]{1,0:T(8,128)S(1)}, u32[]{:S(2)}, u32[]{:S(2)}) collective-permute-start(f32[8,128]{1,0:T(8,128)S(1)} %get-tuple-element.24), channel_id=1, source_target_pairs={{16,0},{32,16},{48,32},{64,48},{80,64},{96,80},{112,96},{128,112},... | collective-permute-start | bytes 12296 | tf_op jit(solution)/shard_map/ppermute | solution.py:372
  14.5 0.0 copy-done.4
  14.5 0.5 %shard_map.79 = (f32[2,4,8,128]{3,2,1,0:T(8,128)S(1)}, f32[5,8,128]{2,1,0:T(8,128)S(1)}, f32[5,8,128]{2,1,0:T(8,128)S(1)}, s32[3,8,128]{2,1,0:T(8,128)S(1)}, f32[3,8,128]{2,1,0:T(8,128)S(1)}) custom-call(f32[3,4,8,128]{3,2,1,0:T(8,128)S(1)} %copy-done, f32[4,8,128]{2,1,0:T(8,128)S(1)} %copy-done.1, f32[4,8,128]{2,1,0:T(8,128)S(1)} %copy-done.2, ...), custom_call_target="tpu_custom_call" | custom-call | tf_op jit(solution)/shard_map/pallas_call | solution.py:322
  15.0 0.0 collective-permute-done.3.left_a
  15.1 0.8 %collective-permute-done.2.from_right = f32[8,128]{1,0:T(8,128)S(1)} collective-permute-done((f32[8,128]{1,0:T(8,128)S(1)}, f32[8,128]{1,0:T(8,128)S(1)}, u32[]{:S(2)}, u32[]{:S(2)}) %collective-permute-start.2) | collective-permute-done | bytes 4128 | tf_op jit(solution)/shard_map/ppermute | solution.py:372
  15.9 0.0 collective-permute-done.4.left_b
  15.9 1.1 %shard_map.80 = (f32[4,8,128]{2,1,0:T(8,128)}, f32[4,8,128]{2,1,0:T(8,128)}, f32[4,8,128]{2,1,0:T(8,128)}) custom-call(f32[2,4,8,128]{3,2,1,0:T(8,128)S(1)} %get-tuple-element.19.inner, f32[5,8,128]{2,1,0:T(8,128)S(1)} %get-tuple-element.20.near, f32[5,8,128]{2,1,0:T(8,128)S(1)} %get-tuple-element.21.near_rows, s32[3,8,128]{2,1,0:T(8,128)S(1)} %get-tuple-element.22.near_off, ...), custom_call_target="tpu_custom_call" | custom-call | tf_op jit(solution)/shard_map/pallas_call | solution.py:322
  (1 shorter events, 0.0 us)
Async XLA Ops:
  0.6 2.7 %copy-start.2 = (f32[4,8,128]{2,1,0:T(8,128)S(1)}, f32[4,8,128]{2,1,0:T(8,128)}, u32[]{:S(2)}) copy-start(f32[4,8,128]{2,1,0:T(8,128)} %old_mm.3) | copy-start | bytes 49156
  0.6 2.7 %copy-start.1 = (f32[4,8,128]{2,1,0:T(8,128)S(1)}, f32[4,8,128]{2,1,0:T(8,128)}, u32[]{:S(2)}) copy-start(f32[4,8,128]{2,1,0:T(8,128)} %old_lm.3) | copy-start | bytes 49156
  0.7 2.7 %copy-start = (f32[3,4,8,128]{3,2,1,0:T(8,128)S(1)}, f32[3,4,8,128]{3,2,1,0:T(8,128)}, u32[]{:S(2)}) copy-start(f32[3,4,8,128]{3,2,1,0:T(8,128)} %vel.3) | copy-start | bytes 147460
  1.6 1.8 %collective-permute-start = (f32[32,128]{1,0:T(8,128)S(1)}, f32[32,128]{1,0:T(8,128)S(1)}, u32[]{:S(2)}, u32[]{:S(2)}) collective-permute-start(f32[32,128]{1,0:T(8,128)S(1)} %get-tuple-element.15), channel_id=1, source_target_pairs={{0,1},{1,0},{2,3},{3,2},{4,5},{5,4},{6,7},{7,6},{8,9},{9,8},{10,11... | collective-permute-start | bytes 49160 | tf_op jit(solution)/shard_map/ppermute | solution.py:355
  1.7 12.8 %copy-start.3 = (s32[3,4,8,128]{3,2,1,0:T(8,128)S(1)}, s32[3,4,8,128]{3,2,1,0:T(8,128)}, u32[]{:S(2)}) copy-start(s32[3,4,8,128]{3,2,1,0:T(8,128)} %offsets.1) | copy-start | bytes 147460
  1.7 12.8 %copy-start.4 = (f32[3,4,8,128]{3,2,1,0:T(8,128)S(1)}, f32[3,4,8,128]{3,2,1,0:T(8,128)}, u32[]{:S(2)}) copy-start(f32[3,4,8,128]{3,2,1,0:T(8,128)} %fractions.1) | copy-start | bytes 147460
  1.7 6.2 %collective-permute-start.1 = (f32[32,128]{1,0:T(8,128)S(1)}, f32[32,128]{1,0:T(8,128)S(1)}, u32[]{:S(2)}, u32[]{:S(2)}) collective-permute-start(f32[32,128]{1,0:T(8,128)S(1)} %get-tuple-element.16), channel_id=1, source_target_pairs={{0,15},{1,2},{2,1},{3,4},{4,3},{5,6},{6,5},{7,8},{8,7},{9,10},{10,... | collective-permute-start | bytes 49160 | tf_op jit(solution)/shard_map/ppermute | solution.py:356
  3.5 12.4 %collective-permute-start.4 = (f32[16,128]{1,0:T(8,128)S(1)}, f32[16,128]{1,0:T(8,128)S(1)}, u32[]{:S(2)}, u32[]{:S(2)}) collective-permute-start(f32[16,128]{1,0:T(8,128)S(1)} %get-tuple-element.26), channel_id=1, source_target_pairs={{0,31},{1,18},{2,17},{3,20},{4,19},{5,22},{6,21},{7,24},{8,23},{9,... | collective-permute-start | bytes 24584 | tf_op jit(solution)/shard_map/ppermute | solution.py:366
  6.0 9.0 %collective-permute-start.3 = (f32[8,128]{1,0:T(8,128)S(1)}, f32[8,128]{1,0:T(8,128)S(1)}, u32[]{:S(2)}, u32[]{:S(2)}) collective-permute-start(f32[8,128]{1,0:T(8,128)S(1)} %get-tuple-element.25), channel_id=1, source_target_pairs={{0,16},{16,32},{32,48},{48,64},{64,80},{80,96},{96,112},{112,128},... | collective-permute-start | bytes 12296 | tf_op jit(solution)/shard_map/ppermute | solution.py:365
  8.0 7.8 %collective-permute-start.2 = (f32[8,128]{1,0:T(8,128)S(1)}, f32[8,128]{1,0:T(8,128)S(1)}, u32[]{:S(2)}, u32[]{:S(2)}) collective-permute-start(f32[8,128]{1,0:T(8,128)S(1)} %get-tuple-element.24), channel_id=1, source_target_pairs={{16,0},{32,16},{48,32},{64,48},{80,64},{96,80},{112,96},{128,112},... | collective-permute-start | bytes 12296 | tf_op jit(solution)/shard_map/ppermute | solution.py:372

commit v7 on v5

--- a/solution.py
+++ b/solution.py
@@ -82,25 +82,43 @@
         outer[plane, 7:8, :] = below[PLANES + plane : PLANES + plane + 1]
 
 
-def first_edges_kernel(got_a, vel, old_lm, old_mm, own_edges, edges, wide, outer):
+def packed_rows(message):
+    upper = lax.broadcasted_iota(jnp.int32, (ROWS, COLS), 0) < ROWS // 2
+
+    def tile(field, z):
+        group, at, last = (field, 2 * z, 6) if field < 3 else (3, LEVELS * (field - 3) + z, 7)
+        rows = message[ROWS * group : ROWS * (group + 1), :]
+        return jnp.where(
+            upper, pltpu.roll(rows, (ROWS - at) % ROWS, 0), pltpu.roll(rows, (last - at) % ROWS, 0)
+        )
+
+    return packed_edges(tile)
+
+
+def first_edges_kernel(got_a, vel, old_lm, old_mm, edges, wide):
     def tile(field, z):
         return vel[field, z] if field < 3 else (old_lm, old_mm)[field - 3][z]
 
-    own_edges[...] = packed_edges(tile)
-    wide[0:ROWS, :] = own_edges[...]
+    own_edges = packed_edges(tile)
+    wide[0:ROWS, :] = own_edges
     wide[ROWS:, :] = jnp.zeros_like(wide[ROWS:, :])
-    fill_outer(got_a[...], got_a[...], outer)
-    edges[0:ROWS, :] = own_edges[...]
-    edges[ROWS:, :] = packed_edges(lambda field, z: outer[LEVELS * field + z])
-
-
-def rows_kernel(got_a, got_b, own_edges, outer, edges):
+    edges[0:ROWS, :] = own_edges
+    edges[ROWS:, :] = packed_rows(got_a)
+
+
+def rows_kernel(got_b, first_edges, edges):
+    even = lax.axis_index("gy") % 2 == 0
+    upper = lax.broadcasted_iota(jnp.int32, (ROWS, COLS), 0) < ROWS // 2
+    a, b = first_edges[ROWS:, :], packed_rows(got_b)
+    edges[0:ROWS, :] = first_edges[0:ROWS, :]
+    edges[ROWS:, :] = jnp.where(even, jnp.where(upper, a, b), jnp.where(upper, b, a))
+
+
+def fill_both(got_a, got_b, outer):
     even = lax.axis_index("gy") % 2 == 0
     above = jnp.where(even, got_a[...], got_b[...])
     below = jnp.where(even, got_b[...], got_a[...])
     fill_outer(above, below, outer)
-    edges[0:ROWS, :] = own_edges[...]
-    edges[ROWS:, :] = packed_edges(lambda field, z: outer[LEVELS * field + z])
 
 
 class Grid:
@@ -266,8 +284,9 @@
 
 
 def inner_kernel(
-    vel, old_lm, old_mm, offsets, fractions, outer, new, near, near_rows, near_off, near_frac
+    vel, old_lm, old_mm, offsets, fractions, got_a, got_b, new, near, near_rows, near_off, near_frac, outer
 ):
+    fill_both(got_a, got_b, outer)
     fields = [vel[c] for c in range(3)] + [old_lm[...], old_mm[...]]
     fields = [(own, outer[LEVELS * f : LEVELS * (f + 1)]) for f, own in enumerate(fields)]
     new[0], new[1] = update(Grid(), fields, [offsets[k] for k in range(3)], [fractions[k] for k in range(3)])
@@ -358,25 +377,24 @@
     got_a = lax.ppermute(msg_a, "gy", even_pairs(ny))
     got_b = lax.ppermute(msg_b, "gy", odd_pairs(ny))
     tile = (ROWS, COLS)
-    own_edges, edges, wide = kernel_call(
+    edges, wide = kernel_call(
         first_edges_kernel,
-        [f32(*tile), f32(2 * ROWS, COLS), f32(3 * ROWS, COLS)],
+        [f32(2 * ROWS, COLS), f32(3 * ROWS, COLS)],
         (got_a, velocity, old_lm, old_mm),
-        scratch=[pltpu.VMEM((PLANES + OLD, *tile), jnp.float32)],
     )
     to_east = [(i, (i + 1) % nx) for i in range(nx)]
     left_a = lax.ppermute(edges, "gx", to_east)
     left_b = lax.ppermute(
         wide, ("gx", "gy"), [(i * ny + j, k * ny + m) for i, k in to_east for j, m in odd_pairs(ny)]
     )
-    outer, edges = kernel_call(
-        rows_kernel, [f32(PLANES + OLD, *tile), f32(2 * ROWS, COLS)], (got_a, got_b, own_edges)
-    )
+    whole = [pltpu.VMEM((PLANES + OLD, *tile), jnp.float32)]
+    (edges,) = kernel_call(rows_kernel, [f32(2 * ROWS, COLS)], (got_b, edges))
     from_right = lax.ppermute(edges, "gx", [(k, i) for i, k in to_east])
     inner, near, near_rows, near_off, near_frac = kernel_call(
         inner_kernel,
         [f32(2, LEVELS, *tile), f32(FIELDS, *tile), f32(FIELDS, *tile), i32(3, *tile), f32(3, *tile)],
-        (velocity, old_lm, old_mm, offsets, fractions, outer),
+        (velocity, old_lm, old_mm, offsets, fractions, got_a, got_b),
+        scratch=whole,
     )
     out = f32(LEVELS, *tile)
     return tuple(

time: 17 us -> 17 us (level)
  no operation moved by 1% of the time
where the time goes in v7:
time: 17 us; the launch traced here: 16.9 us
  starting transfers between devices  12.7 us (75%)
  Pallas kernels  2.6 us (15%)
  waiting for transfers between devices  0.85 us (5%)
  between operations  0.73 us (4%)
    ppermute x1, starting transfers between devices, body(): from_right = lax.ppermute(edges, 'gx', [(k, i) for i, k in to_east])  6.5 us
    pallas_call x5, Pallas kernels, kernel_call(): pl.pallas_call(kernel, out_shape=outs, in_specs=[VMEM] * len(args) if spa...  2.6 us
    ppermute x1, starting transfers between devices, body(): lax.ppermute(wide, ('gx', 'gy'), [(i * ny + j, k * ny + m) for i, k in to...  2.53 us
    ppermute x1, starting transfers between devices, body(): left_a = lax.ppermute(edges, 'gx', to_east)  1.92 us
    ppermute x1, starting transfers between devices, body(): got_b = lax.ppermute(msg_b, 'gy', odd_pairs(ny))  1.63 us
    ppermute x1, waiting for transfers between devices, body(): from_right = lax.ppermute(edges, 'gx', [(k, i) for i, k in to_east])  0.84 us
  transfers between devices with their start and end apart: 5, of which 1 were waited for; matrix products, arithmetic and copies ran while one was open for 0% of the time, Pallas kernels for 4%

profile of v7, /device:TPU:2, one launch (start us, length us, event | category | flops | bytes accessed | tf_op | source)
XLA Modules:
  0.0 16.9 jit_solution(959977615922396019)
XLA Ops:
  0.6 0.0 copy-start.2
  0.6 0.0 copy-start.1
  0.7 0.0 copy-start
  0.7 0.9 %shard_map.76 = (f32[32,128]{1,0:T(8,128)S(1)}, f32[32,128]{1,0:T(8,128)S(1)}) custom-call(f32[3,4,8,128]{3,2,1,0:T(8,128)} %vel.3, f32[4,8,128]{2,1,0:T(8,128)} %old_lm.3, f32[4,8,128]{2,1,0:T(8,128)} %old_mm.3), custom_call_target="tpu_custom_call" | custom-call | tf_op jit(solution)/shard_map/pallas_call | solution.py:344
  1.6 0.1 collective-permute-start
  1.7 0.0 copy-start.3
  1.7 0.0 copy-start.4
  1.7 1.6 %collective-permute-start.1 = (f32[32,128]{1,0:T(8,128)S(1)}, f32[32,128]{1,0:T(8,128)S(1)}, u32[]{:S(2)}, u32[]{:S(2)}) collective-permute-start(f32[32,128]{1,0:T(8,128)S(1)} %get-tuple-element.13), channel_id=1, source_target_pairs={{0,15},{1,2},{2,1},{3,4},{4,3},{5,6},{6,5},{7,8},{8,7},{9,10},{10,... | collective-permute-start | bytes 49160 | tf_op jit(solution)/shard_map/ppermute | solution.py:378
  3.3 0.0 collective-permute-done.got_a
  3.3 0.0 copy-done.2
  3.3 0.0 copy-done.1
  3.3 0.0 copy-done
  3.4 0.1 shard_map.78
  3.5 2.5 %collective-permute-start.4 = (f32[24,128]{1,0:T(8,128)S(1)}, f32[24,128]{1,0:T(8,128)S(1)}, u32[]{:S(2)}, u32[]{:S(2)}) collective-permute-start(f32[24,128]{1,0:T(8,128)S(1)} %get-tuple-element.20), channel_id=1, source_target_pairs={{0,31},{1,18},{2,17},{3,20},{4,19},{5,22},{6,21},{7,24},{8,23},{9,... | collective-permute-start | bytes 36872 | tf_op jit(solution)/shard_map/ppermute | solution.py:387
  6.0 1.9 %collective-permute-start.3 = (f32[16,128]{1,0:T(8,128)S(1)}, f32[16,128]{1,0:T(8,128)S(1)}, u32[]{:S(2)}, u32[]{:S(2)}) collective-permute-start(f32[16,128]{1,0:T(8,128)S(1)} %get-tuple-element.19.first_edges), channel_id=1, source_target_pairs={{0,16},{16,32},{32,48},{48,64},{64,80},{80,96},{96,112},{112,128},... | collective-permute-start | bytes 24584 | tf_op jit(solution)/shard_map/ppermute | solution.py:386
  7.9 0.0 collective-permute-done.1.got_b
  7.9 0.1 shard_map.79
  8.0 6.5 %collective-permute-start.2 = (f32[16,128]{1,0:T(8,128)S(1)}, f32[16,128]{1,0:T(8,128)S(1)}, u32[]{:S(2)}, u32[]{:S(2)}) collective-permute-start(f32[16,128]{1,0:T(8,128)S(1)} %shard_map.79), channel_id=1, source_target_pairs={{16,0},{32,16},{48,32},{64,48},{80,64},{96,80},{112,96},{128,112},... | collective-permute-start | bytes 24584 | tf_op jit(solution)/shard_map/ppermute | solution.py:392
  14.5 0.0 copy-done.3
  14.5 0.5 %shard_map.77 = (f32[2,4,8,128]{3,2,1,0:T(8,128)S(1)}, f32[5,8,128]{2,1,0:T(8,128)S(1)}, f32[5,8,128]{2,1,0:T(8,128)S(1)}, s32[3,8,128]{2,1,0:T(8,128)S(1)}, f32[3,8,128]{2,1,0:T(8,128)S(1)}) custom-call(f32[3,4,8,128]{3,2,1,0:T(8,128)S(1)} %copy-done, f32[4,8,128]{2,1,0:T(8,128)S(1)} %copy-done.1, f32[4,8,128]{2,1,0:T(8,128)S(1)} %copy-done.2, ...), custom_call_target="tpu_custom_call" | custom-call | tf_op jit(solution)/shard_map/pallas_call | solution.py:344
  15.0 0.0 collective-permute-done.3.left_a
  15.0 0.8 %collective-permute-done.2.from_right = f32[16,128]{1,0:T(8,128)S(1)} collective-permute-done((f32[16,128]{1,0:T(8,128)S(1)}, f32[16,128]{1,0:T(8,128)S(1)}, u32[]{:S(2)}, u32[]{:S(2)}) %collective-permute-start.2) | collective-permute-done | bytes 8224 | tf_op jit(solution)/shard_map/ppermute | solution.py:392
  15.9 0.0 collective-permute-done.4.left_b
  15.9 1.0 %shard_map.80 = (f32[4,8,128]{2,1,0:T(8,128)}, f32[4,8,128]{2,1,0:T(8,128)}, f32[4,8,128]{2,1,0:T(8,128)}) custom-call(f32[2,4,8,128]{3,2,1,0:T(8,128)S(1)} %get-tuple-element.14.inner, f32[5,8,128]{2,1,0:T(8,128)S(1)} %get-tuple-element.15.near, f32[5,8,128]{2,1,0:T(8,128)S(1)} %get-tuple-element.16.near_rows, s32[3,8,128]{2,1,0:T(8,128)S(1)} %get-tuple-element.17.near_off, ...), custom_call_target="tpu_custom_call" | custom-call | tf_op jit(solution)/shard_map/pallas_call | solution.py:344
  (1 shorter events, 0.0 us)
Async XLA Ops:
  0.6 2.7 %copy-start.2 = (f32[4,8,128]{2,1,0:T(8,128)S(1)}, f32[4,8,128]{2,1,0:T(8,128)}, u32[]{:S(2)}) copy-start(f32[4,8,128]{2,1,0:T(8,128)} %old_mm.3) | copy-start | bytes 49156
  0.6 2.7 %copy-start.1 = (f32[4,8,128]{2,1,0:T(8,128)S(1)}, f32[4,8,128]{2,1,0:T(8,128)}, u32[]{:S(2)}) copy-start(f32[4,8,128]{2,1,0:T(8,128)} %old_lm.3) | copy-start | bytes 49156
  0.7 2.7 %copy-start = (f32[3,4,8,128]{3,2,1,0:T(8,128)S(1)}, f32[3,4,8,128]{3,2,1,0:T(8,128)}, u32[]{:S(2)}) copy-start(f32[3,4,8,128]{3,2,1,0:T(8,128)} %vel.3) | copy-start | bytes 147460
  1.6 1.8 %collective-permute-start = (f32[32,128]{1,0:T(8,128)S(1)}, f32[32,128]{1,0:T(8,128)S(1)}, u32[]{:S(2)}, u32[]{:S(2)}) collective-permute-start(f32[32,128]{1,0:T(8,128)S(1)} %get-tuple-element.12), channel_id=1, source_target_pairs={{0,1},{1,0},{2,3},{3,2},{4,5},{5,4},{6,7},{7,6},{8,9},{9,8},{10,11... | collective-permute-start | bytes 49160 | tf_op jit(solution)/shard_map/ppermute | solution.py:377
  1.7 12.8 %copy-start.3 = (s32[3,4,8,128]{3,2,1,0:T(8,128)S(1)}, s32[3,4,8,128]{3,2,1,0:T(8,128)}, u32[]{:S(2)}) copy-start(s32[3,4,8,128]{3,2,1,0:T(8,128)} %offsets.1) | copy-start | bytes 147460
  1.7 12.8 %copy-start.4 = (f32[3,4,8,128]{3,2,1,0:T(8,128)S(1)}, f32[3,4,8,128]{3,2,1,0:T(8,128)}, u32[]{:S(2)}) copy-start(f32[3,4,8,128]{3,2,1,0:T(8,128)} %fractions.1) | copy-start | bytes 147460
  1.7 6.2 %collective-permute-start.1 = (f32[32,128]{1,0:T(8,128)S(1)}, f32[32,128]{1,0:T(8,128)S(1)}, u32[]{:S(2)}, u32[]{:S(2)}) collective-permute-start(f32[32,128]{1,0:T(8,128)S(1)} %get-tuple-element.13), channel_id=1, source_target_pairs={{0,15},{1,2},{2,1},{3,4},{4,3},{5,6},{6,5},{7,8},{8,7},{9,10},{10,... | collective-permute-start | bytes 49160 | tf_op jit(solution)/shard_map/ppermute | solution.py:378
  3.5 12.4 %collective-permute-start.4 = (f32[24,128]{1,0:T(8,128)S(1)}, f32[24,128]{1,0:T(8,128)S(1)}, u32[]{:S(2)}, u32[]{:S(2)}) collective-permute-start(f32[24,128]{1,0:T(8,128)S(1)} %get-tuple-element.20), channel_id=1, source_target_pairs={{0,31},{1,18},{2,17},{3,20},{4,19},{5,22},{6,21},{7,24},{8,23},{9,... | collective-permute-start | bytes 36872 | tf_op jit(solution)/shard_map/ppermute | solution.py:387
  6.0 9.0 %collective-permute-start.3 = (f32[16,128]{1,0:T(8,128)S(1)}, f32[16,128]{1,0:T(8,128)S(1)}, u32[]{:S(2)}, u32[]{:S(2)}) collective-permute-start(f32[16,128]{1,0:T(8,128)S(1)} %get-tuple-element.19.first_edges), channel_id=1, source_target_pairs={{0,16},{16,32},{32,48},{48,64},{64,80},{80,96},{96,112},{112,128},... | collective-permute-start | bytes 24584 | tf_op jit(solution)/shard_map/ppermute | solution.py:386
  8.0 7.9 %collective-permute-start.2 = (f32[16,128]{1,0:T(8,128)S(1)}, f32[16,128]{1,0:T(8,128)S(1)}, u32[]{:S(2)}, u32[]{:S(2)}) collective-permute-start(f32[16,128]{1,0:T(8,128)S(1)} %shard_map.79), channel_id=1, source_target_pairs={{16,0},{32,16},{48,32},{64,48},{80,64},{96,80},{112,96},{128,112},... | collective-permute-start | bytes 24584 | tf_op jit(solution)/shard_map/ppermute | solution.py:392

commit v8 on v7

--- a/solution.py
+++ b/solution.py
@@ -34,11 +34,6 @@
             moved = pltpu.roll(tile(field, z), first + (2 if field < 3 else 1), 1)
             packed = moved if packed is None else jnp.where(lane >= first, moved, packed)
     return packed
-
-
-def from_right_mask():
-    lane = lanes() % GROUP
-    return jnp.where(lane < 12, lane % 4, 2 * (lane % 2)) >= 2
 
 
 def edge_domain(tile):
@@ -301,7 +296,6 @@
 def edge_kernel(
     inner, near, near_rows, near_off, near_frac, from_right, left_a, left_b, new_lm, new_mm, coefficient
 ):
-    right = from_right_mask()
     place = lanes() % GROUP
     is_right, is_left = (place == 4) | (place == 5), (place == 6) | (place == 7)
     even = lax.axis_index("gy") % 2 == 0
@@ -311,13 +305,13 @@
     from_left = (left_a[0:ROWS, :], corners)
     pairs = [[], []]
     for half, own in enumerate((near, near_rows)):
-        halo = jnp.where(right, from_right[half * ROWS : (half + 1) * ROWS, :], from_left[half])
+        east, west = from_right[half * ROWS : (half + 1) * ROWS, :], from_left[half]
         for field in range(FIELDS):
             first = 4 * field if field < 3 else 12 + 2 * (field - 3)
             to_right = (4 - first - (2 if field < 3 else 1)) % COLS
             to_left = ((6 if field < 3 else 7) - first) % COLS
-            tile = jnp.where(is_left, pltpu.roll(halo, to_left, 1), own[field])
-            pairs[half].append(jnp.where(is_right, pltpu.roll(halo, to_right, 1), tile))
+            tile = jnp.where(is_left, pltpu.roll(west, to_left, 1), own[field])
+            pairs[half].append(jnp.where(is_right, pltpu.roll(east, to_right, 1), tile))
     fields = list(zip(*pairs))
     edge = update(EdgeGrid(), fields, [near_off[k] for k in range(3)], [near_frac[k] for k in range(3)])
     lane = lanes()

time: 17 us -> 17 us (level)
  no operation moved by 1% of the time
where the time goes in v8:
time: 17 us; the launch traced here: 16.9 us
  starting transfers between devices  12.7 us (75%)
  Pallas kernels  2.6 us (15%)
  waiting for transfers between devices  0.85 us (5%)
  between operations  0.73 us (4%)
    ppermute x1, starting transfers between devices, body(): from_right = lax.ppermute(edges, 'gx', [(k, i) for i, k in to_east])  6.5 us
    pallas_call x5, Pallas kernels, kernel_call(): pl.pallas_call(kernel, out_shape=outs, in_specs=[VMEM] * len(args) if spa...  2.6 us
    ppermute x1, starting transfers between devices, body(): lax.ppermute(wide, ('gx', 'gy'), [(i * ny + j, k * ny + m) for i, k in to...  2.53 us
    ppermute x1, starting transfers between devices, body(): left_a = lax.ppermute(edges, 'gx', to_east)  1.92 us
    ppermute x1, starting transfers between devices, body(): got_b = lax.ppermute(msg_b, 'gy', odd_pairs(ny))  1.63 us
    ppermute x1, waiting for transfers between devices, body(): from_right = lax.ppermute(edges, 'gx', [(k, i) for i, k in to_east])  0.84 us
  transfers between devices with their start and end apart: 5, of which 1 were waited for; matrix products, arithmetic and copies ran while one was open for 0% of the time, Pallas kernels for 4%

profile of v8, /device:TPU:2, one launch (start us, length us, event | category | flops | bytes accessed | tf_op | source)
XLA Modules:
  0.0 16.9 jit_solution(3705765581221819528)
XLA Ops:
  0.6 0.0 copy-start.2
  0.6 0.0 copy-start.1
  0.7 0.0 copy-start
  0.7 0.9 %shard_map.76 = (f32[32,128]{1,0:T(8,128)S(1)}, f32[32,128]{1,0:T(8,128)S(1)}) custom-call(f32[3,4,8,128]{3,2,1,0:T(8,128)} %vel.3, f32[4,8,128]{2,1,0:T(8,128)} %old_lm.3, f32[4,8,128]{2,1,0:T(8,128)} %old_mm.3), custom_call_target="tpu_custom_call" | custom-call | tf_op jit(solution)/shard_map/pallas_call | solution.py:338
  1.6 0.1 collective-permute-start
  1.7 0.0 copy-start.3
  1.7 0.0 copy-start.4
  1.7 1.6 %collective-permute-start.1 = (f32[32,128]{1,0:T(8,128)S(1)}, f32[32,128]{1,0:T(8,128)S(1)}, u32[]{:S(2)}, u32[]{:S(2)}) collective-permute-start(f32[32,128]{1,0:T(8,128)S(1)} %get-tuple-element.13), channel_id=1, source_target_pairs={{0,15},{1,2},{2,1},{3,4},{4,3},{5,6},{6,5},{7,8},{8,7},{9,10},{10,... | collective-permute-start | bytes 49160 | tf_op jit(solution)/shard_map/ppermute | solution.py:372
  3.3 0.0 collective-permute-done.got_a
  3.3 0.0 copy-done.2
  3.3 0.0 copy-done.1
  3.3 0.0 copy-done
  3.4 0.1 shard_map.78
  3.5 2.5 %collective-permute-start.4 = (f32[24,128]{1,0:T(8,128)S(1)}, f32[24,128]{1,0:T(8,128)S(1)}, u32[]{:S(2)}, u32[]{:S(2)}) collective-permute-start(f32[24,128]{1,0:T(8,128)S(1)} %get-tuple-element.20), channel_id=1, source_target_pairs={{0,31},{1,18},{2,17},{3,20},{4,19},{5,22},{6,21},{7,24},{8,23},{9,... | collective-permute-start | bytes 36872 | tf_op jit(solution)/shard_map/ppermute | solution.py:381
  6.0 1.9 %collective-permute-start.3 = (f32[16,128]{1,0:T(8,128)S(1)}, f32[16,128]{1,0:T(8,128)S(1)}, u32[]{:S(2)}, u32[]{:S(2)}) collective-permute-start(f32[16,128]{1,0:T(8,128)S(1)} %get-tuple-element.19.first_edges), channel_id=1, source_target_pairs={{0,16},{16,32},{32,48},{48,64},{64,80},{80,96},{96,112},{112,128},... | collective-permute-start | bytes 24584 | tf_op jit(solution)/shard_map/ppermute | solution.py:380
  7.9 0.0 collective-permute-done.1.got_b
  7.9 0.1 shard_map.79
  8.0 6.5 %collective-permute-start.2 = (f32[16,128]{1,0:T(8,128)S(1)}, f32[16,128]{1,0:T(8,128)S(1)}, u32[]{:S(2)}, u32[]{:S(2)}) collective-permute-start(f32[16,128]{1,0:T(8,128)S(1)} %shard_map.79), channel_id=1, source_target_pairs={{16,0},{32,16},{48,32},{64,48},{80,64},{96,80},{112,96},{128,112},... | collective-permute-start | bytes 24584 | tf_op jit(solution)/shard_map/ppermute | solution.py:386
  14.5 0.0 copy-done.3
  14.5 0.5 %shard_map.77 = (f32[2,4,8,128]{3,2,1,0:T(8,128)S(1)}, f32[5,8,128]{2,1,0:T(8,128)S(1)}, f32[5,8,128]{2,1,0:T(8,128)S(1)}, s32[3,8,128]{2,1,0:T(8,128)S(1)}, f32[3,8,128]{2,1,0:T(8,128)S(1)}) custom-call(f32[3,4,8,128]{3,2,1,0:T(8,128)S(1)} %copy-done, f32[4,8,128]{2,1,0:T(8,128)S(1)} %copy-done.1, f32[4,8,128]{2,1,0:T(8,128)S(1)} %copy-done.2, ...), custom_call_target="tpu_custom_call" | custom-call | tf_op jit(solution)/shard_map/pallas_call | solution.py:338
  15.0 0.0 collective-permute-done.3.left_a
  15.0 0.8 %collective-permute-done.2.from_right = f32[16,128]{1,0:T(8,128)S(1)} collective-permute-done((f32[16,128]{1,0:T(8,128)S(1)}, f32[16,128]{1,0:T(8,128)S(1)}, u32[]{:S(2)}, u32[]{:S(2)}) %collective-permute-start.2) | collective-permute-done | bytes 8224 | tf_op jit(solution)/shard_map/ppermute | solution.py:386
  15.9 0.0 collective-permute-done.4.left_b
  15.9 1.0 %shard_map.80 = (f32[4,8,128]{2,1,0:T(8,128)}, f32[4,8,128]{2,1,0:T(8,128)}, f32[4,8,128]{2,1,0:T(8,128)}) custom-call(f32[2,4,8,128]{3,2,1,0:T(8,128)S(1)} %get-tuple-element.14.inner, f32[5,8,128]{2,1,0:T(8,128)S(1)} %get-tuple-element.15.near, f32[5,8,128]{2,1,0:T(8,128)S(1)} %get-tuple-element.16.near_rows, s32[3,8,128]{2,1,0:T(8,128)S(1)} %get-tuple-element.17.near_off, ...), custom_call_target="tpu_custom_call" | custom-call | tf_op jit(solution)/shard_map/pallas_call | solution.py:338
  (1 shorter events, 0.0 us)
Async XLA Ops:
  0.6 2.7 %copy-start.2 = (f32[4,8,128]{2,1,0:T(8,128)S(1)}, f32[4,8,128]{2,1,0:T(8,128)}, u32[]{:S(2)}) copy-start(f32[4,8,128]{2,1,0:T(8,128)} %old_mm.3) | copy-start | bytes 49156
  0.6 2.7 %copy-start.1 = (f32[4,8,128]{2,1,0:T(8,128)S(1)}, f32[4,8,128]{2,1,0:T(8,128)}, u32[]{:S(2)}) copy-start(f32[4,8,128]{2,1,0:T(8,128)} %old_lm.3) | copy-start | bytes 49156
  0.7 2.7 %copy-start = (f32[3,4,8,128]{3,2,1,0:T(8,128)S(1)}, f32[3,4,8,128]{3,2,1,0:T(8,128)}, u32[]{:S(2)}) copy-start(f32[3,4,8,128]{3,2,1,0:T(8,128)} %vel.3) | copy-start | bytes 147460
  1.6 1.8 %collective-permute-start = (f32[32,128]{1,0:T(8,128)S(1)}, f32[32,128]{1,0:T(8,128)S(1)}, u32[]{:S(2)}, u32[]{:S(2)}) collective-permute-start(f32[32,128]{1,0:T(8,128)S(1)} %get-tuple-element.12), channel_id=1, source_target_pairs={{0,1},{1,0},{2,3},{3,2},{4,5},{5,4},{6,7},{7,6},{8,9},{9,8},{10,11... | collective-permute-start | bytes 49160 | tf_op jit(solution)/shard_map/ppermute | solution.py:371
  1.7 12.8 %copy-start.3 = (s32[3,4,8,128]{3,2,1,0:T(8,128)S(1)}, s32[3,4,8,128]{3,2,1,0:T(8,128)}, u32[]{:S(2)}) copy-start(s32[3,4,8,128]{3,2,1,0:T(8,128)} %offsets.1) | copy-start | bytes 147460
  1.7 12.8 %copy-start.4 = (f32[3,4,8,128]{3,2,1,0:T(8,128)S(1)}, f32[3,4,8,128]{3,2,1,0:T(8,128)}, u32[]{:S(2)}) copy-start(f32[3,4,8,128]{3,2,1,0:T(8,128)} %fractions.1) | copy-start | bytes 147460
  1.7 6.2 %collective-permute-start.1 = (f32[32,128]{1,0:T(8,128)S(1)}, f32[32,128]{1,0:T(8,128)S(1)}, u32[]{:S(2)}, u32[]{:S(2)}) collective-permute-start(f32[32,128]{1,0:T(8,128)S(1)} %get-tuple-element.13), channel_id=1, source_target_pairs={{0,15},{1,2},{2,1},{3,4},{4,3},{5,6},{6,5},{7,8},{8,7},{9,10},{10,... | collective-permute-start | bytes 49160 | tf_op jit(solution)/shard_map/ppermute | solution.py:372
  3.5 12.4 %collective-permute-start.4 = (f32[24,128]{1,0:T(8,128)S(1)}, f32[24,128]{1,0:T(8,128)S(1)}, u32[]{:S(2)}, u32[]{:S(2)}) collective-permute-start(f32[24,128]{1,0:T(8,128)S(1)} %get-tuple-element.20), channel_id=1, source_target_pairs={{0,31},{1,18},{2,17},{3,20},{4,19},{5,22},{6,21},{7,24},{8,23},{9,... | collective-permute-start | bytes 36872 | tf_op jit(solution)/shard_map/ppermute | solution.py:381
  6.0 9.0 %collective-permute-start.3 = (f32[16,128]{1,0:T(8,128)S(1)}, f32[16,128]{1,0:T(8,128)S(1)}, u32[]{:S(2)}, u32[]{:S(2)}) collective-permute-start(f32[16,128]{1,0:T(8,128)S(1)} %get-tuple-element.19.first_edges), channel_id=1, source_target_pairs={{0,16},{16,32},{32,48},{48,64},{64,80},{80,96},{96,112},{112,128},... | collective-permute-start | bytes 24584 | tf_op jit(solution)/shard_map/ppermute | solution.py:380
  8.0 7.9 %collective-permute-start.2 = (f32[16,128]{1,0:T(8,128)S(1)}, f32[16,128]{1,0:T(8,128)S(1)}, u32[]{:S(2)}, u32[]{:S(2)}) collective-permute-start(f32[16,128]{1,0:T(8,128)S(1)} %shard_map.79), channel_id=1, source_target_pairs={{16,0},{32,16},{48,32},{64,48},{80,64},{96,80},{112,96},{128,112},... | collective-permute-start | bytes 24584 | tf_op jit(solution)/shard_map/ppermute | solution.py:386
